TPU v7x, 128 devices: a whole 4x4x4 slice. The times are simulated.
128 devices in a mesh: dp: 2 (over core), seq: 64 (over z, x, y).
Axes of the slice: x: 4, y: 4, z: 4, core: 2. Of those that a mesh axis runs over, the one named last changes fastest.
Arguments:
- queries: bfloat16 [512, 64, 2048], P(('dp', 'seq'))
- outputs: bfloat16 [512, 64, 2048], P(('dp', 'seq')), may hold values from -6 to 6
- out_grad: bfloat16 [512, 64, 2048], P(('dp', 'seq')), may hold values from -6 to 6
- keys: bfloat16 [512, 128, 2048], P(('dp', 'seq'))
- values: bfloat16 [512, 128, 2048], P(('dp', 'seq')), may hold values from -6 to 6
- owner: int32 [512, 2], P(('dp', 'seq')), may hold values from 0 to 63, as said below
- slot: int32 [512, 2], P(('dp', 'seq')), may hold values from 0 to 3
- pos_bias: float32 [1024, 128], replicated, may hold values from -6 to 6
Outputs:
- query_grad: bfloat16 [512, 64, 2048], P(('dp', 'seq'))
- key_grad: float32 [512, 128, 2048], P(('dp', 'seq'))
- value_grad: float32 [512, 128, 2048], P(('dp', 'seq'))
- bias_grad: float32 [1024, 128], P(('dp', 'seq'))
Inputs may be any that keep to these rules, and one draw needn't show every extreme that they name: A neighbour's owner is at most 2 positions away, cyclically along seq, from the device that holds the span. From the spans of one device at most 2 neighbours have the same owner, and in every draw some owner receives exactly 2 from some device.
All inputs are finite; a program needn't handle non-finite values.
Results may differ from a plain program's by a relative error of at most 0.0048.
Values may be sent and summed in bfloat16 or wider, within the bound.
A program may use at most 192 MiB of HBM per device.

v0:
```python
import jax
import jax.numpy as jnp
from jax import lax
from jax.sharding import PartitionSpec as P

REACH = 2
CAP = 2


def passed_along(block, axis, distance):
    devices = range(lax.axis_size(axis))
    route = [((i - distance) % len(devices), i) for i in devices]
    return lax.ppermute(block, axis, route)


def accumulate(block_count, requested_list, piece_list):
    total = None
    for requested, pieces in zip(requested_list, piece_list):
        onehot = (jnp.arange(block_count, dtype=jnp.int32)[:, None] == requested[None, :]).astype(
            jnp.float32
        )
        flat_pieces = pieces.reshape(pieces.shape[0], -1)
        added = jnp.dot(
            onehot, flat_pieces, precision=lax.Precision.HIGHEST, preferred_element_type=jnp.float32
        )
        total = added if total is None else total + added
    return total.reshape((block_count,) + piece_list[0].shape[1:])


def select_rows(position, lane_width, piece_list, out_type):
    total = None
    for lane_id, pieces in enumerate(piece_list):
        local_rows = position - lane_id * lane_width
        onehot = (local_rows[:, None] == jnp.arange(lane_width, dtype=jnp.int32)[None, :]).astype(
            pieces.dtype
        )
        flat_pieces = pieces.reshape(pieces.shape[0], -1)
        picked = jnp.dot(onehot, flat_pieces, preferred_element_type=jnp.float32)
        total = picked if total is None else total + picked
    return total.astype(out_type).reshape((position.shape[0],) + piece_list[0].shape[1:])


def per_device(queries, outputs, out_grad, keys, values, owner, slot, pos_bias):
    span_count, row_count, feat_width = queries.shape
    block_count, block_len, _ = keys.shape
    head_count = pos_bias.shape[0] // row_count
    head_size = feat_width // head_count
    scaling = head_size ** (-0.5)
    seq_count = lax.axis_size("seq")
    local_seq = lax.axis_index("seq")
    lane_total = 2 * REACH + 1
    slot_total = lane_total * CAP
    pair_count = 2 * span_count
    lane_of = (owner.reshape(pair_count) - local_seq + REACH) % seq_count - REACH + REACH
    member = (lane_of[:, None] == jnp.arange(lane_total, dtype=jnp.int32)[None, :]).astype(
        jnp.int32
    )
    earlier = jnp.cumsum(member, axis=0) - member
    slot_rank = jnp.sum(earlier * member, axis=1)
    position = lane_of * CAP + slot_rank
    slot_table = (position[None, :] == jnp.arange(slot_total, dtype=jnp.int32)[:, None]).astype(
        jnp.int32
    )
    filled = jnp.sum(slot_table, axis=1)
    chosen = jnp.sum(slot_table * jnp.arange(pair_count, dtype=jnp.int32)[None, :], axis=1)
    wanted = jnp.where(filled > 0, slot.reshape(pair_count)[chosen], block_count)
    wanted = wanted.reshape(lane_total, CAP)
    incoming = []
    for lane_id in range(lane_total):
        hop_now = lane_id - REACH
        incoming.append(
            wanted[lane_id] if hop_now == 0 else passed_along(wanted[lane_id], "seq", hop_now)
        )
    query_heads = queries.reshape(span_count, row_count, head_count, head_size)
    grad_heads = out_grad.reshape(span_count, row_count, head_count, head_size)
    products = (out_grad.astype(jnp.float32) * outputs.astype(jnp.float32)).reshape(
        span_count, row_count, head_count, head_size
    )
    row_terms = jnp.transpose(jnp.sum(products, axis=-1), (0, 2, 1))
    bias_three = pos_bias.reshape(head_count, row_count, block_len)
    key_pieces = []
    value_pieces = []
    fetched_keys = []
    fetched_values = []
    for lane_id in range(lane_total):
        hop_now = lane_id - REACH
        safe_ids = jnp.minimum(incoming[lane_id], block_count - 1)
        served = (keys[safe_ids], values[safe_ids])
        arrived = served if hop_now == 0 else passed_along((served[0], served[1]), "seq", -hop_now)
        fetched_keys.append(arrived[0])
        fetched_values.append(arrived[1])
    pair_keys = select_rows(position, CAP, fetched_keys, jnp.bfloat16).reshape(
        span_count, 2 * block_len, head_count, head_size
    )
    pair_values = select_rows(position, CAP, fetched_values, jnp.bfloat16).reshape(
        span_count, 2 * block_len, head_count, head_size
    )
    bias_pair = jnp.concatenate([bias_three, bias_three], axis=-1)
    scores = (
        jnp.einsum("cihd,cjhd->chij", query_heads, pair_keys, preferred_element_type=jnp.float32)
        * scaling
        + bias_pair[None]
    )
    highest = jnp.max(scores, axis=-1, keepdims=True)
    log_total = highest[..., 0] + jnp.log(jnp.sum(jnp.exp(scores - highest), axis=-1))
    weights = jnp.exp(scores - log_total[..., None])
    weights_low = weights.astype(jnp.bfloat16)
    grad_weights = jnp.einsum(
        "cihd,cjhd->chij", grad_heads, pair_values, preferred_element_type=jnp.float32
    )
    grad_scores = weights * (grad_weights - row_terms[..., None])
    grad_low = grad_scores.astype(jnp.bfloat16)
    query_full = (
        jnp.einsum("chij,cjhd->cihd", grad_low, pair_keys, preferred_element_type=jnp.float32)
        * scaling
    )
    query_grad = query_full.reshape(span_count, row_count, feat_width).astype(jnp.bfloat16)
    pair_key_grad = (
        jnp.einsum("chij,cihd->cjhd", grad_low, query_heads, preferred_element_type=jnp.float32)
        * scaling
    ).reshape(pair_count, block_len, feat_width)
    pair_value_grad = jnp.einsum(
        "chij,cihd->cjhd", weights_low, grad_heads, preferred_element_type=jnp.float32
    ).reshape(pair_count, block_len, feat_width)
    bias_local = jnp.sum(
        grad_scores.reshape(span_count, head_count, row_count, 2, block_len), axis=(0, 3)
    )
    slot_keys = (
        jnp.zeros((slot_total, block_len, feat_width), jnp.float32).at[position].set(pair_key_grad)
    )
    slot_values = (
        jnp.zeros((slot_total, block_len, feat_width), jnp.float32)
        .at[position]
        .set(pair_value_grad)
    )
    slot_keys = slot_keys.reshape(lane_total, CAP, block_len, feat_width)
    slot_values = slot_values.reshape(lane_total, CAP, block_len, feat_width)
    for lane_id in range(lane_total):
        hop_now = lane_id - REACH
        outgoing = (slot_keys[lane_id], slot_values[lane_id])
        returned = (
            outgoing if hop_now == 0 else passed_along((outgoing[0], outgoing[1]), "seq", hop_now)
        )
        key_pieces.append(returned[0])
        value_pieces.append(returned[1])
    key_grad = accumulate(block_count, incoming, key_pieces)
    value_grad = accumulate(block_count, incoming, value_pieces)
    bias_flat = bias_local.reshape(head_count * row_count, block_len)
    bias_grad = lax.psum_scatter(bias_flat, ("dp", "seq"), scatter_dimension=0, tiled=True)
    return (query_grad, key_grad, value_grad, bias_grad)


def solution(mesh):
    in_specs = (
        P(("dp", "seq"), None, None),
        P(("dp", "seq"), None, None),
        P(("dp", "seq"), None, None),
        P(("dp", "seq"), None, None),
        P(("dp", "seq"), None, None),
        P(("dp", "seq"), None),
        P(("dp", "seq"), None),
        P(),
    )
    out_specs = (
        P(("dp", "seq"), None, None),
        P(("dp", "seq"), None, None),
        P(("dp", "seq"), None, None),
        P(("dp", "seq"), None),
    )
    return jax.shard_map(
        per_device, mesh=mesh, in_specs=in_specs, out_specs=out_specs, check_vma=False
    )
```

profile of v0, /device:TPU:1, one launch (start us, length us, event | category | flops | bytes accessed | tf_op | source)
XLA Modules:
  0.0 783.3 jit_solution(10614555808182499585)
XLA Ops:
  10.3 3.8 collective-permute-start.6
  14.0 5.6 collective-permute-start.2
  28.4 4.6 fusion.42
  34.6 2.9 collective-permute-start.7
  39.5 4.6 collective-permute-start.3
  47.2 3.2 gather_fusion.8
  52.8 4.6 fusion.41
  57.4 3.2 gather_fusion.10
  60.6 3.2 gather_fusion.7
  63.8 3.2 gather_fusion.6
  68.6 3.2 gather_fusion.9
  71.9 6.6 collective-permute-start.5
  79.0 25.4 %collective-permute-done.7 = bf16[2,128,2048]{2,1,0:T(8,128)(2,1)} collective-permute-done((bf16[2,128,2048]{2,1,0:T(8,128)(2,1)}, bf16[2,128,2048]{2,1,0:T(8,128)(2,1)}, u32[]{:S(2)}, u32[]{:S(2)}) %collective-permute-start.7) | collective-permute-done | bytes 1048608 | tf_op jit(solution)/shard_map/ppermute | solution.py:13
  107.2 21.5 %collective-permute-start.8 = (bf16[2,128,2048]{2,1,0:T(8,128)(2,1)}, bf16[2,128,2048]{2,1,0:T(8,128)(2,1)}, u32[]{:S(2)}, u32[]{:S(2)}) collective-permute-start(bf16[2,128,2048]{2,1,0:T(8,128)(2,1)} %gather_fusion.6), channel_id=1, source_target_pairs={{62,0},{63,1},{0,2},{1,3},{2,4},{3,5},{4,6},{5,7},{6,8},{7,9},{8,1... | collective-permute-start | bytes 3145736 | tf_op jit(solution)/shard_map/ppermute | solution.py:13
  131.2 5.3 collective-permute-start.10
  140.9 4.6 fusion.3
  148.8 7.1 fusion.4
  155.9 6.1 reshape_reshape.6
  161.9 14.5 %collective-permute-done.11 = bf16[2,128,2048]{2,1,0:T(8,128)(2,1)} collective-permute-done((bf16[2,128,2048]{2,1,0:T(8,128)(2,1)}, bf16[2,128,2048]{2,1,0:T(8,128)(2,1)}, u32[]{:S(2)}, u32[]{:S(2)}) %collective-permute-start.11) | collective-permute-done | bytes 1048608 | tf_op jit(solution)/shard_map/ppermute | solution.py:13
  181.0 3.4 copy.87
  184.5 4.7 fusion.39
  189.2 4.6 fusion.43
  193.7 12.5 %collective-permute-done.10 = bf16[2,128,2048]{2,1,0:T(8,128)(2,1)} collective-permute-done((bf16[2,128,2048]{2,1,0:T(8,128)(2,1)}, bf16[2,128,2048]{2,1,0:T(8,128)(2,1)}, u32[]{:S(2)}, u32[]{:S(2)}) %collective-permute-start.10) | collective-permute-done | bytes 1048608 | tf_op jit(solution)/shard_map/ppermute | solution.py:13
  206.2 3.3 copy.90
  216.0 8.1 %copy.76 = f32[4,256,16,128]{3,2,1,0:T(8,128)} copy(f32[4,256,16,128]{3,1,2,0:T(8,128)S(1)} %convolution_bitcast_fusion) | data formatting | bytes 16777216 | tf_op jit(solution)/shard_map/chij,cihd->cjhd/transpose | solution.py:122
  224.1 9.3 %reshape.418 = f32[8,128,2048]{2,1,0:T(8,128)} reshape(f32[4,256,16,128]{3,2,1,0:T(8,128)} %copy.76) | data formatting | bytes 16777216 | tf_op jit(solution)/shard_map/reshape | solution.py:124
  233.4 5.3 broadcast.407.clone
  238.7 15.4 %scatter_fusion.1 = f32[10,128,2048]{2,1,0:T(8,128)} fusion(f32[10,128,2048]{2,1,0:T(8,128)} %broadcast.407.clone, s32[8]{0:T(128)S(1)} %fusion.77, f32[8,128,2048]{2,1,0:T(8,128)} %reshape.418), kind=kCustom, calls=%fused_computation.12 | custom fusion | bytes 25165856 | tf_op jit(solution)/shard_map/scatter | solution.py:134
  254.1 8.4 %fusion.79 = (f32[2,128,2048]{2,1,0:T(8,128)}, f32[2,128,2048]{2,1,0:T(8,128)}, f32[1,2,128,2048]{3,2,1,0:T(8,128)}, f32[2,128,2048]{2,1,0:T(8,128)}, f32[2,128,2048]{2,1,0:T(8,128)}) fusion(f32[10,128,2048]{2,1,0:T(8,128)} %scatter_fusion.1), kind=kLoop, calls=%fused_computation.151 | loop fusion | bytes 20971520 | tf_op jit(solution)/shard_map/slice | solution.py:140
  262.5 7.0 collective-permute-start.19
  269.5 5.4 collective-permute-start.17
  277.7 10.5 %fusion.1 = f32[8,262144]{1,0:T(8,128)} fusion(f32[8,262144]{1,0:T(8,128)} %fusion.41, f32[8,262144]{1,0:T(8,128)} %fusion.43, bf16[2,262144]{1,0:T(2,128)(2,1)S(1)} %bitcast.168, s32[8]{0:T(128)S(1)} %get-tuple-element.7), kind=kOutput, calls=%fused_computation.16 | convolution fusion | flops 12582928 | bytes 26214432 | tf_op jit(solution)/shard_map/dot_general | solution.py:38
  288.2 7.1 fusion.5
  295.3 6.0 reshape_reshape.7
  301.4 5.8 fusion.82
  308.5 8.1 %copy.74 = f32[4,256,16,128]{3,2,1,0:T(8,128)} copy(f32[4,256,16,128]{3,1,2,0:T(8,128)S(1)} %multiply_bitcast_fusion) | data formatting | bytes 16777216 | tf_op jit(solution)/shard_map/mul | solution.py:119
  316.6 9.3 %reshape.410 = f32[8,128,2048]{2,1,0:T(8,128)} reshape(f32[4,256,16,128]{3,2,1,0:T(8,128)} %copy.74) | data formatting | bytes 16777216 | tf_op jit(solution)/shard_map/reshape | solution.py:121
  325.9 5.3 broadcast.407.clone.1
  331.2 15.4 %scatter_fusion = f32[10,128,2048]{2,1,0:T(8,128)} fusion(f32[10,128,2048]{2,1,0:T(8,128)} %broadcast.407.clone.1, s32[8]{0:T(128)S(1)} %fusion.77, f32[8,128,2048]{2,1,0:T(8,128)} %reshape.410), kind=kCustom, calls=%fused_computation.11 | custom fusion | bytes 25165856 | tf_op jit(solution)/shard_map/scatter | solution.py:129
  346.6 8.4 %fusion.80 = (f32[2,128,2048]{2,1,0:T(8,128)}, f32[2,128,2048]{2,1,0:T(8,128)}, f32[1,2,128,2048]{3,2,1,0:T(8,128)}, f32[2,128,2048]{2,1,0:T(8,128)}, f32[2,128,2048]{2,1,0:T(8,128)}) fusion(f32[10,128,2048]{2,1,0:T(8,128)} %scatter_fusion), kind=kLoop, calls=%fused_computation.152 | loop fusion | bytes 20971520 | tf_op jit(solution)/shard_map/slice | solution.py:140
  355.7 55.9 %collective-permute-start.13 = (f32[2,128,2048]{2,1,0:T(8,128)}, f32[2,128,2048]{2,1,0:T(8,128)}, u32[]{:S(2)}, u32[]{:S(2)}) collective-permute-start(f32[2,128,2048]{2,1,0:T(8,128)} %get-tuple-element.16), channel_id=1, source_target_pairs={{1,0},{2,1},{3,2},{4,3},{5,4},{6,5},{7,6},{8,7},{9,8},{10,9},{11,1... | collective-permute-start | bytes 6291464 | tf_op jit(solution)/shard_map/ppermute | solution.py:13
  411.5 38.9 %collective-permute-done.17 = f32[2,128,2048]{2,1,0:T(8,128)} collective-permute-done((f32[2,128,2048]{2,1,0:T(8,128)}, f32[2,128,2048]{2,1,0:T(8,128)}, u32[]{:S(2)}, u32[]{:S(2)}) %collective-permute-start.17) | collective-permute-done | bytes 2097184 | tf_op jit(solution)/shard_map/ppermute | solution.py:13
  453.3 3.7 fusion.26
  459.9 2.9 copy.95
  466.8 5.5 fusion.48
  472.3 5.7 fusion.49
  478.0 217.9 %all-reduce.3.cloned.1.call-done = f32[1024,128]{1,0:T(8,128)} async-done(((f32[1024,128]{1,0:T(8,128)}), f32[1024,128]{1,0:T(8,128)}) %all-reduce.3.cloned.1.call-update) | async-done | bytes 524304
  697.2 3.2 copy.103
  700.4 3.2 copy.100
  703.6 3.2 copy.99
  706.8 3.2 copy.102
  710.1 3.2 copy.97
  713.3 3.2 copy.94
  716.5 5.0 copy.93
  721.5 4.6 copy.96
  726.1 4.2 fusion.46
  730.3 5.5 fusion.50
  735.8 4.2 fusion.47
  740.0 4.2 fusion.51
  744.2 6.8 fusion.7
  751.1 6.4 fusion.6
  757.5 5.1 fusion.9
  762.6 5.3 fusion.8
  768.0 8.2 %copy_bitcast_fusion = (f32[4,128,2048]{2,1,0:T(8,128)}, f32[4,128,2048]{2,1,0:T(8,128)}) fusion(f32[1,4,128,2048]{3,1,2,0:T(4,128)S(1)} %bitcast.148, f32[1,4,128,2048]{3,1,2,0:T(4,128)S(1)} %bitcast.149), kind=kLoop, calls=%fused_computation.32 | loop fusion | bytes 16777216 | tf_op jit(solution)/shard_map/reshape | solution.py:27
  (148 shorter events, 62.8 us)
Async XLA Ops:
  7.2 14.7 %copy-start = (bf16[4,128,2048]{2,1,0:T(8,128)(2,1)S(1)}, bf16[4,128,2048]{2,1,0:T(8,128)(2,1)}, u32[]{:S(2)}) copy-start(bf16[4,128,2048]{2,1,0:T(8,128)(2,1)} %param.11) | copy-start | bytes 6291460
  7.2 18.6 %copy-start.12 = (bf16[4,64,2048]{2,1,0:T(8,128)(2,1)S(1)}, bf16[4,64,2048]{2,1,0:T(8,128)(2,1)}, u32[]{:S(2)}) copy-start(bf16[4,64,2048]{2,1,0:T(8,128)(2,1)} %param.10) | copy-start | bytes 3145732
  7.2 688.7 %all-reduce.3.cloned.1.call-start = ((), (), s32[]{:S(2)}) async-start(), calls=%async_computation | async-start | bytes 1048576
  10.3 22.7 %collective-permute-start.6 = (s32[2]{0:T(128)S(1)}, s32[2]{0:T(128)S(1)}, u32[]{:S(2)}, u32[]{:S(2)}) collective-permute-start(s32[2]{0:T(128)S(1)} %get-tuple-element.20), channel_id=1, source_target_pairs={{62,0},{63,1},{0,2},{1,3},{2,4},{3,5},{4,6},{5,7},{6,8},{7,9},{8,1... | collective-permute-start | bytes 32 | tf_op jit(solution)/shard_map/ppermute | solution.py:13
  14.0 23.4 %collective-permute-start.2 = (s32[2]{0:T(128)S(1)}, s32[2]{0:T(128)S(1)}, u32[]{:S(2)}, u32[]{:S(2)}) collective-permute-start(s32[2]{0:T(128)S(1)} %get-tuple-element.22), channel_id=1, source_target_pairs={{1,0},{2,1},{3,2},{4,3},{5,4},{6,5},{7,6},{8,7},{9,8},{10,9},{11,1... | collective-permute-start | bytes 32 | tf_op jit(solution)/shard_map/ppermute | solution.py:13
  19.6 24.6 %collective-permute-start = (s32[2]{0:T(128)S(1)}, s32[2]{0:T(128)S(1)}, u32[]{:S(2)}, u32[]{:S(2)}) collective-permute-start(s32[2]{0:T(128)S(1)} %get-tuple-element.23), channel_id=1, source_target_pairs={{2,0},{3,1},{4,2},{5,3},{6,4},{7,5},{8,6},{9,7},{10,8},{11,9},{12,... | collective-permute-start | bytes 32 | tf_op jit(solution)/shard_map/ppermute | solution.py:13
  21.9 45.1 %collective-permute-start.4 = (s32[2]{0:T(128)S(1)}, s32[2]{0:T(128)S(1)}, u32[]{:S(2)}, u32[]{:S(2)}) collective-permute-start(s32[2]{0:T(128)S(1)} %get-tuple-element.21), channel_id=1, source_target_pairs={{63,0},{0,1},{1,2},{2,3},{3,4},{4,5},{5,6},{6,7},{7,8},{8,9},{9,10... | collective-permute-start | bytes 32 | tf_op jit(solution)/shard_map/ppermute | solution.py:13
  34.6 69.8 %collective-permute-start.7 = (bf16[2,128,2048]{2,1,0:T(8,128)(2,1)}, bf16[2,128,2048]{2,1,0:T(8,128)(2,1)}, u32[]{:S(2)}, u32[]{:S(2)}) collective-permute-start(bf16[2,128,2048]{2,1,0:T(8,128)(2,1)} %gather_fusion.5), channel_id=1, source_target_pairs={{2,0},{3,1},{4,2},{5,3},{6,4},{7,5},{8,6},{9,7},{10,8},{11,9},{12,... | collective-permute-start | bytes 3145736 | tf_op jit(solution)/shard_map/ppermute | solution.py:13
  37.4 0.5 copy-start.24
  39.5 67.6 %collective-permute-start.3 = (bf16[2,128,2048]{2,1,0:T(8,128)(2,1)}, bf16[2,128,2048]{2,1,0:T(8,128)(2,1)}, u32[]{:S(2)}, u32[]{:S(2)}) collective-permute-start(bf16[2,128,2048]{2,1,0:T(8,128)(2,1)} %gather_fusion.2), channel_id=1, source_target_pairs={{63,0},{0,1},{1,2},{2,3},{3,4},{4,5},{5,6},{6,7},{7,8},{8,9},{9,10... | collective-permute-start | bytes 3145736 | tf_op jit(solution)/shard_map/ppermute | solution.py:13
  44.2 1.6 copy-start.22
  45.8 85.4 %collective-permute-start.1 = (bf16[2,128,2048]{2,1,0:T(8,128)(2,1)}, bf16[2,128,2048]{2,1,0:T(8,128)(2,1)}, u32[]{:S(2)}, u32[]{:S(2)}) collective-permute-start(bf16[2,128,2048]{2,1,0:T(8,128)(2,1)} %gather_fusion.1), channel_id=1, source_target_pairs={{62,0},{63,1},{0,2},{1,3},{2,4},{3,5},{4,6},{5,7},{6,8},{7,9},{8,1... | collective-permute-start | bytes 3145736 | tf_op jit(solution)/shard_map/ppermute | solution.py:13
  67.0 64.2 %copy-start.20 = (s32[2]{0:T(128)}, s32[2]{0:T(128)S(1)}, u32[]{:S(2)}) copy-start(s32[2]{0:T(128)S(1)} %collective-permute-done.4) | copy-start | bytes 28
  71.9 75.8 %collective-permute-start.5 = (bf16[2,128,2048]{2,1,0:T(8,128)(2,1)}, bf16[2,128,2048]{2,1,0:T(8,128)(2,1)S(1)}, u32[]{:S(2)}, u32[]{:S(2)}) collective-permute-start(bf16[2,128,2048]{2,1,0:T(8,128)(2,1)} %gather_fusion.4), channel_id=1, source_target_pairs={{1,0},{2,1},{3,2},{4,3},{5,4},{6,5},{7,6},{8,7},{9,8},{10,9},{11,1... | collective-permute-start | bytes 3145736 | tf_op jit(solution)/shard_map/ppermute | solution.py:13
  78.5 97.9 %collective-permute-start.11 = (bf16[2,128,2048]{2,1,0:T(8,128)(2,1)}, bf16[2,128,2048]{2,1,0:T(8,128)(2,1)}, u32[]{:S(2)}, u32[]{:S(2)}) collective-permute-start(bf16[2,128,2048]{2,1,0:T(8,128)(2,1)} %gather_fusion.10), channel_id=1, source_target_pairs={{2,0},{3,1},{4,2},{5,3},{6,4},{7,5},{8,6},{9,7},{10,8},{11,9},{12,... | collective-permute-start | bytes 3145736 | tf_op jit(solution)/shard_map/ppermute | solution.py:13
  104.4 74.3 %collective-permute-start.9 = (bf16[2,128,2048]{2,1,0:T(8,128)(2,1)}, bf16[2,128,2048]{2,1,0:T(8,128)(2,1)}, u32[]{:S(2)}, u32[]{:S(2)}) collective-permute-start(bf16[2,128,2048]{2,1,0:T(8,128)(2,1)} %gather_fusion.7), channel_id=1, source_target_pairs={{63,0},{0,1},{1,2},{2,3},{3,4},{4,5},{5,6},{6,7},{7,8},{8,9},{9,10... | collective-permute-start | bytes 3145736 | tf_op jit(solution)/shard_map/ppermute | solution.py:13
  107.2 73.9 %collective-permute-start.8 = (bf16[2,128,2048]{2,1,0:T(8,128)(2,1)}, bf16[2,128,2048]{2,1,0:T(8,128)(2,1)}, u32[]{:S(2)}, u32[]{:S(2)}) collective-permute-start(bf16[2,128,2048]{2,1,0:T(8,128)(2,1)} %gather_fusion.6), channel_id=1, source_target_pairs={{62,0},{63,1},{0,2},{1,3},{2,4},{3,5},{4,6},{5,7},{6,8},{7,9},{8,1... | collective-permute-start | bytes 3145736 | tf_op jit(solution)/shard_map/ppermute | solution.py:13
  128.7 11.4 %slice-start.2 = ((s8[8388608]{0:T(1024)(128)(4,1)}), s8[4194304]{0:T(1024)(128)(4,1)S(1)}, s32[]{:S(2)}) async-start(s8[8388608]{0:T(1024)(128)(4,1)} %bitcast.146), calls=%async_computation.3 | async-start | bytes 8388608
  131.2 75.0 %collective-permute-start.10 = (bf16[2,128,2048]{2,1,0:T(8,128)(2,1)}, bf16[2,128,2048]{2,1,0:T(8,128)(2,1)}, u32[]{:S(2)}, u32[]{:S(2)}) collective-permute-start(bf16[2,128,2048]{2,1,0:T(8,128)(2,1)} %gather_fusion.9), channel_id=1, source_target_pairs={{1,0},{2,1},{3,2},{4,3},{5,4},{6,5},{7,6},{8,7},{9,8},{10,9},{11,1... | collective-permute-start | bytes 3145736 | tf_op jit(solution)/shard_map/ppermute | solution.py:13
  138.8 2.2 slice-start.3
  189.2 20.3 %copy-start.8 = (bf16[4,256,16,128]{3,2,1,0:T(8,128)(2,1)S(1)}, bf16[4,256,16,128]{3,2,1,0:T(8,128)(2,1)}, u32[]{:S(2)}) copy-start(bf16[4,256,16,128]{3,2,1,0:T(8,128)(2,1)} %reshape_reshape.6) | copy-start | bytes 12582916
  189.2 20.3 %copy-start.16 = (bf16[4,64,2048]{2,1,0:T(8,128)(2,1)S(1)}, bf16[4,64,2048]{2,1,0:T(8,128)(2,1)}, u32[]{:S(2)}) copy-start(bf16[4,64,2048]{2,1,0:T(8,128)(2,1)} %param.8) | copy-start | bytes 3145732
  211.3 2.1 copy-start.4
  211.3 2.1 copy-start.13
  254.1 23.6 %copy-start.14 = (bf16[1,2,128,2048]{3,1,2,0:T(2,128)(2,1)S(1)}, bf16[1,2,128,2048]{3,1,2,0:T(2,128)(2,1)}, u32[]{:S(2)}) copy-start(bf16[1,2,128,2048]{3,1,2,0:T(2,128)(2,1)} %copy.87) | copy-start | bytes 3145732
  254.1 34.1 %slice-start = ((s8[8388608]{0:T(1024)(128)(4,1)}), s8[4194304]{0:T(1024)(128)(4,1)S(1)}, s32[]{:S(2)}) async-start(s8[8388608]{0:T(1024)(128)(4,1)} %bitcast.144), calls=%async_computation.1 | async-start | bytes 8388608
  262.5 93.1 %collective-permute-start.19 = (f32[2,128,2048]{2,1,0:T(8,128)}, f32[2,128,2048]{2,1,0:T(8,128)}, u32[]{:S(2)}, u32[]{:S(2)}) collective-permute-start(f32[2,128,2048]{2,1,0:T(8,128)} %get-tuple-element.9), channel_id=1, source_target_pairs={{62,0},{63,1},{0,2},{1,3},{2,4},{3,5},{4,6},{5,7},{6,8},{7,9},{8,1... | collective-permute-start | bytes 6291464 | tf_op jit(solution)/shard_map/ppermute | solution.py:13
  269.5 180.9 %collective-permute-start.17 = (f32[2,128,2048]{2,1,0:T(8,128)}, f32[2,128,2048]{2,1,0:T(8,128)}, u32[]{:S(2)}, u32[]{:S(2)}) collective-permute-start(f32[2,128,2048]{2,1,0:T(8,128)} %get-tuple-element.11), channel_id=1, source_target_pairs={{1,0},{2,1},{3,2},{4,3},{5,4},{6,5},{7,6},{8,7},{9,8},{10,9},{11,1... | collective-permute-start | bytes 6291464 | tf_op jit(solution)/shard_map/ppermute | solution.py:13
  274.9 176.7 %collective-permute-start.16 = (f32[2,128,2048]{2,1,0:T(8,128)}, f32[2,128,2048]{2,1,0:T(8,128)}, u32[]{:S(2)}, u32[]{:S(2)}) collective-permute-start(f32[2,128,2048]{2,1,0:T(8,128)} %get-tuple-element.12), channel_id=1, source_target_pairs={{2,0},{3,1},{4,2},{5,3},{6,4},{7,5},{8,6},{9,7},{10,8},{11,9},{12,... | collective-permute-start | bytes 6291464 | tf_op jit(solution)/shard_map/ppermute | solution.py:13
  277.7 10.5 %slice-start.1 = ((s8[8388608]{0:T(1024)(128)(4,1)}), s8[4194304]{0:T(1024)(128)(4,1)S(1)}, s32[]{:S(2)}) async-start(s8[8388608]{0:T(1024)(128)(4,1)} %bitcast.144), calls=%async_computation.2 | async-start | bytes 8388608
  277.7 10.5 %copy-start.15 = (bf16[1,2,128,2048]{3,1,2,0:T(2,128)(2,1)S(1)}, bf16[1,2,128,2048]{3,1,2,0:T(2,128)(2,1)}, u32[]{:S(2)}) copy-start(bf16[1,2,128,2048]{3,1,2,0:T(2,128)(2,1)} %copy.90) | copy-start | bytes 3145732
  301.4 5.8 copy-start.17
  301.4 405.5 %collective-permute-start.18 = (f32[2,128,2048]{2,1,0:T(8,128)}, f32[2,128,2048]{2,1,0:T(8,128)}, u32[]{:S(2)}, u32[]{:S(2)}) collective-permute-start(f32[2,128,2048]{2,1,0:T(8,128)} %get-tuple-element.8), channel_id=1, source_target_pairs={{63,0},{0,1},{1,2},{2,3},{3,4},{4,5},{5,6},{6,7},{7,8},{8,9},{9,10... | collective-permute-start | bytes 6291464 | tf_op jit(solution)/shard_map/ppermute | solution.py:13
  307.2 1.3 copy-start.18
  346.6 106.7 %copy-start.19 = (bf16[4,16,64,256]{3,2,1,0:T(8,128)(2,1)S(1)}, bf16[4,16,64,256]{3,2,1,0:T(8,128)(2,1)}, u32[]{:S(2)}) copy-start(bf16[4,16,64,256]{3,2,1,0:T(8,128)(2,1)} %copy-done.18) | copy-start | bytes 6291460
  355.0 355.1 %collective-permute-start.15 = (f32[2,128,2048]{2,1,0:T(8,128)}, f32[2,128,2048]{2,1,0:T(8,128)}, u32[]{:S(2)}, u32[]{:S(2)}) collective-permute-start(f32[2,128,2048]{2,1,0:T(8,128)} %get-tuple-element.14), channel_id=1, source_target_pairs={{62,0},{63,1},{0,2},{1,3},{2,4},{3,5},{4,6},{5,7},{6,8},{7,9},{8,1... | collective-permute-start | bytes 6291464 | tf_op jit(solution)/shard_map/ppermute | solution.py:13
  355.7 357.6 %collective-permute-start.13 = (f32[2,128,2048]{2,1,0:T(8,128)}, f32[2,128,2048]{2,1,0:T(8,128)}, u32[]{:S(2)}, u32[]{:S(2)}) collective-permute-start(f32[2,128,2048]{2,1,0:T(8,128)} %get-tuple-element.16), channel_id=1, source_target_pairs={{1,0},{2,1},{3,2},{4,3},{5,4},{6,5},{7,6},{8,7},{9,8},{10,9},{11,1... | collective-permute-start | bytes 6291464 | tf_op jit(solution)/shard_map/ppermute | solution.py:13
  450.5 266.0 %collective-permute-start.12 = (f32[2,128,2048]{2,1,0:T(8,128)}, f32[2,128,2048]{2,1,0:T(8,128)}, u32[]{:S(2)}, u32[]{:S(2)}) collective-permute-start(f32[2,128,2048]{2,1,0:T(8,128)} %get-tuple-element.17), channel_id=1, source_target_pairs={{2,0},{3,1},{4,2},{5,3},{6,4},{7,5},{8,6},{9,7},{10,8},{11,9},{12,... | collective-permute-start | bytes 6291464 | tf_op jit(solution)/shard_map/ppermute | solution.py:13
  451.6 269.9 %collective-permute-start.14 = (f32[2,128,2048]{2,1,0:T(8,128)}, f32[2,128,2048]{2,1,0:T(8,128)}, u32[]{:S(2)}, u32[]{:S(2)}) collective-permute-start(f32[2,128,2048]{2,1,0:T(8,128)} %get-tuple-element.13), channel_id=1, source_target_pairs={{63,0},{0,1},{1,2},{2,3},{3,4},{4,5},{5,6},{6,7},{7,8},{8,9},{9,10... | collective-permute-start | bytes 6291464 | tf_op jit(solution)/shard_map/ppermute | solution.py:13
  453.3 5.0 copy-start.10
  457.0 2.9 copy-start.11
  466.8 5.5 copy-start.9
  726.1 4.2 copy-start.25
  740.0 4.2 copy-start.3
  740.0 4.2 copy-start.23
  744.2 6.9 copy-start.21
  751.1 6.4 copy-start.2
  751.1 6.4 copy-start.6
  757.5 5.1 copy-start.7
  762.6 5.3 copy-start.5
  768.0 8.3 %copy-start.1 = (bf16[4,128,2048]{2,1,0:T(8,128)(2,1)S(1)}, bf16[4,128,2048]{2,1,0:T(8,128)(2,1)}, u32[]{:S(2)}) copy-start(bf16[4,128,2048]{2,1,0:T(8,128)(2,1)} %param.11) | copy-start | bytes 6291460
Sparse Core Ops, SparseCore 0:
  466.9 228.9 all-reduce.2
where the time goes:
time: 793 us; the launch traced here: 783 us
  waiting for transfers between devices  311 us (39%)
  local copies, waits for them, and re-layouts  203 us (26%)
  starting transfers between devices  127 us (16%)
  matrix products  118 us (15%)
  between operations  14.8 us (2%)
  other arithmetic  8.6 us (1%)
    unnamed x2, waiting for transfers between devices  218 us
    ppermute x20, starting transfers between devices, passed_along(): return lax.ppermute(block, axis, route)  127 us
    ppermute x20, waiting for transfers between devices, passed_along(): return lax.ppermute(block, axis, route)  93.3 us
    unnamed x83, local copies, waits for them, and re-layouts  61.9 us
    dot_general x10, matrix products, accumulate(): jnp.dot(onehot, flat_pieces, precision=lax.Precision.HIGHEST, preferred_e...  52.9 us
    dot_general x10, matrix products, select_rows(): picked = jnp.dot(onehot, flat_pieces, preferred_element_type=jnp.float32)  50.3 us
    gather x10, local copies, waits for them, and re-layouts, per_device(): served = (keys[safe_ids], values[safe_ids])  24 us
    slice x2, local copies, waits for them, and re-layouts, per_device(): outgoing = (slot_keys[lane_id], slot_values[lane_id])  16.9 us
  transfers between devices with their start and end apart: 21, of which 7 were waited for; matrix products, arithmetic and copies ran while one was open for 27% of the time, Pallas kernels for 0%

commit v1 on v0

v1 whole, which is shorter than its diff:
```python
import functools

import jax
import jax.numpy as jnp
from jax import lax
from jax.experimental import pallas as pl
from jax.experimental.pallas import tpu as pltpu
from jax.sharding import PartitionSpec as P

REACH = 2
CAP = 2
LANES = 2 * REACH + 1
SLOTS = LANES * CAP
HEADS_PER_PART = 2
AHEAD = 2
UNUSED = 1e30
MESH = pl.DeviceIdType.MESH
REMOTE = tuple(lane for lane in range(LANES) if lane != REACH)


def rows_dot(a, b):
    return lax.dot_general(a, b, (((1,), (1,)), ((), ())), preferred_element_type=jnp.float32)


def plain_dot(a, b):
    return jnp.dot(a, b, preferred_element_type=jnp.float32)


def kernel(
    cfg,
    owner_ref,
    slot_ref,
    q_ref,
    o_ref,
    g_ref,
    k_ref,
    v_ref,
    bias_ref,
    qg_ref,
    kg_ref,
    vg_ref,
    bg_ref,
    meta_send,
    meta_recv,
    mask_row,
    mask_col,
    terms,
    span_send,
    span_recv,
    part_send,
    part_recv,
    part_pick,
    total_send,
    total_recv,
    tops,
    exps,
    grads,
    w_wide,
    d_wide,
    d_tall,
    dq_send,
    dq_recv,
    dq_pick,
    kg_hold,
    vg_hold,
    bias_sum,
    core_recv,
    z_send,
    z_recv,
    x_send,
    x_recv,
    y_send,
    y_recv,
    meta_ss,
    meta_rs,
    span_ss,
    span_rs,
    part_ss,
    part_rs,
    total_ss,
    total_rs,
    dq_ss,
    dq_rs,
    hold_sem,
    core_ss,
    core_rs,
    ring_ss,
    ring_rs,
):
    spans, rows, seq_count, parts, blocks, scaling = cfg
    width = HEADS_PER_PART * 128
    pairs = 2 * spans
    dp = lax.axis_index("dp")
    me = lax.axis_index("seq")
    at_z, at_x, at_y = me // 16, (me // 4) % 4, me % 4

    def owner_at(lane):
        return (dp, lax.rem(me + (lane - REACH) + seq_count, seq_count))

    def asker_at(lane):
        return (dp, lax.rem(me - (lane - REACH) + seq_count, seq_count))

    ring_peers = []
    for step in (1, 2, 3):
        ring_peers.append((dp, ((at_z + step) % 4) * 16 + at_x * 4 + at_y))
        ring_peers.append((dp, at_z * 16 + ((at_x + step) % 4) * 4 + at_y))
        ring_peers.append((dp, at_z * 16 + at_x * 4 + (at_y + step) % 4))
    greeted = [owner_at(lane) for lane in REMOTE] + ring_peers + [(1 - dp, me)]
    barrier = pltpu.get_barrier_semaphore()
    for device in greeted:
        pl.semaphore_signal(barrier, inc=1, device_id=device, device_id_type=MESH)

    lane_of = [
        lax.rem(owner_ref[p // 2, p % 2] - me + REACH + seq_count, seq_count) for p in range(pairs)
    ]
    place = []
    for p in range(pairs):
        rank = jnp.int32(0)
        for other in range(p):
            rank = rank + jnp.where(lane_of[other] == lane_of[p], 1, 0)
        place.append(jnp.minimum(lane_of[p] * CAP + rank, SLOTS - 1))
    chosen, filled, block_id, partner = [], [], [], []
    for s in range(SLOTS):
        pick, used, block, mate = jnp.int32(0), jnp.int32(0), jnp.int32(0), jnp.int32(0)
        for p in range(pairs):
            hit = place[p] == s
            pick = jnp.where(hit, p // 2, pick)
            used = jnp.where(hit, 1, used)
            block = jnp.where(hit, slot_ref[p // 2, p % 2], block)
            mate = jnp.where(hit, place[p ^ 1], mate)
        chosen.append(pick)
        filled.append(used)
        block_id.append(block)
        partner.append((mate // 2) * 2 + (mate + s) % 2)

    lane_id = lax.broadcasted_iota(jnp.int32, (8, 128), 1)
    row_id = lax.broadcasted_iota(jnp.int32, (8, 128), 0)
    first_half = lane_id < rows

    def meta_copy(lane):
        return pltpu.make_async_remote_copy(
            src_ref=meta_send.at[lane],
            dst_ref=meta_recv.at[lane],
            send_sem=meta_ss.at[lane],
            recv_sem=meta_rs.at[lane],
            device_id=owner_at(lane),
            device_id_type=MESH,
        )

    def span_copy(part, lane):
        return pltpu.make_async_remote_copy(
            src_ref=span_send.at[part, lane],
            dst_ref=span_recv.at[part, lane],
            send_sem=span_ss.at[part, lane],
            recv_sem=span_rs.at[part, lane],
            device_id=owner_at(lane),
            device_id_type=MESH,
        )

    def part_copy(part, lane):
        return pltpu.make_async_remote_copy(
            src_ref=part_send.at[part, lane],
            dst_ref=part_recv.at[part, lane],
            send_sem=part_ss.at[part, lane],
            recv_sem=part_rs.at[part, lane],
            device_id=asker_at(lane),
            device_id_type=MESH,
        )

    def total_copy(part, lane):
        return pltpu.make_async_remote_copy(
            src_ref=total_send.at[part, lane],
            dst_ref=total_recv.at[part, lane],
            send_sem=total_ss.at[part, lane],
            recv_sem=total_rs.at[part, lane],
            device_id=owner_at(lane),
            device_id_type=MESH,
        )

    def dq_copy(part, lane):
        return pltpu.make_async_remote_copy(
            src_ref=dq_send.at[part, lane],
            dst_ref=dq_recv.at[part, lane],
            send_sem=dq_ss.at[part, lane],
            recv_sem=dq_rs.at[part, lane],
            device_id=asker_at(lane),
            device_id_type=MESH,
        )

    def hold_copy(part, which):
        held, out = ((kg_hold, kg_ref), (vg_hold, vg_ref))[which]
        columns = pl.ds(pl.multiple_of(part * width, width), width)
        return pltpu.make_async_copy(held.at[part], out.at[:, columns], hold_sem.at[which, part])

    def pack(part):
        columns = pl.ds(pl.multiple_of(part * width, width), width)
        for lane in range(LANES):
            target = span_recv if lane == REACH else span_send
            for half in range(CAP):
                span = chosen[lane * CAP + half]
                target[part, lane, 0, half * rows : (half + 1) * rows, :] = q_ref[span, :, columns]
                target[part, lane, 1, half * rows : (half + 1) * rows, :] = g_ref[span, :, columns]

    def send_spans(part):
        for lane in REMOTE:
            span_copy(part, lane).start()

    for lane in range(LANES):
        tile = jnp.where(first_half, block_id[2 * lane], block_id[2 * lane + 1])
        target = meta_recv if lane == REACH else meta_send
        target[lane] = tile.astype(jnp.float32)
    pack(0)
    pl.semaphore_wait(barrier, len(greeted))
    for lane in REMOTE:
        meta_copy(lane).start()
    send_spans(0)

    def pack_and_send(part, carry):
        pack(part)
        send_spans(part)
        return carry

    lax.fori_loop(1, AHEAD, pack_and_send, 0)

    def span_terms(span, carry):
        wide_lane = lax.broadcasted_iota(jnp.int32, (rows, 128), 1)
        gathered = jnp.zeros((rows, 128), jnp.float32)
        for head in range(parts * HEADS_PER_PART):
            cols = slice(head * 128, (head + 1) * 128)
            product = g_ref[span, :, cols].astype(jnp.float32) * o_ref[span, :, cols].astype(
                jnp.float32
            )
            gathered = jnp.where(
                wide_lane == head, jnp.sum(product, axis=1, keepdims=True), gathered
            )
        turned = jnp.concatenate([gathered, gathered], axis=0).T
        for part in range(parts):
            first = part * HEADS_PER_PART
            terms[span, part, HEADS_PER_PART : 2 * HEADS_PER_PART, :] = turned[
                first : first + HEADS_PER_PART, :
            ]
        return carry

    lax.fori_loop(0, spans, span_terms, 0)

    for lane in REMOTE:
        meta_copy(lane).wait_recv()
    for lane in range(LANES):
        wide = jnp.broadcast_to(meta_recv[lane, 0:1, :], (128, 128))
        tall = wide.T
        for b in range(blocks):
            mask_row[lane, b] = jnp.where(wide[0:16] == b, 1.0, 0.0).astype(jnp.bfloat16)
            mask_col[lane, b] = jnp.where(tall == b, 1.0, 0.0).astype(jnp.bfloat16)

    def picked(products, ids):
        result = products[0:128]
        for b in range(1, blocks):
            result = jnp.where(ids == b, products[b * 128 : (b + 1) * 128], result)
        return result

    def score(part):
        slot_now = lax.rem(part, 3)
        for lane in REMOTE:
            span_copy(part, lane).wait_recv()
        for sub in range(HEADS_PER_PART):
            cols = pl.ds(pl.multiple_of(part * width + sub * 128, 128), 128)
            inner = slice(sub * 128, (sub + 1) * 128)
            key_rows = k_ref[:, cols]
            value_rows = v_ref[:, cols]
            bias_rows = bias_ref[
                pl.ds(pl.multiple_of((part * HEADS_PER_PART + sub) * rows, rows), rows), :
            ]
            bias_turned = jnp.concatenate([bias_rows, bias_rows], axis=0).T
            for lane in range(LANES):
                ids = meta_recv[lane, 0:1, :]
                scores = (
                    picked(rows_dot(key_rows, span_recv[part, lane, 0, :, inner]), ids) * scaling
                    + bias_turned
                )
                top = jnp.max(scores, axis=0, keepdims=True)
                lifted = jnp.exp(scores - top)
                exps[slot_now, sub, lane] = lifted
                tops[slot_now, lane, sub : sub + 1, :] = top
                target = part_recv if lane == REACH else part_send
                target[part, lane, sub : sub + 1, :] = top + jnp.log(
                    jnp.sum(lifted, axis=0, keepdims=True)
                )
                grads[slot_now, sub, lane] = picked(
                    rows_dot(value_rows, span_recv[part, lane, 1, :, inner]), ids
                )
        for lane in REMOTE:
            part_copy(part, lane).start()

    def combine(part):
        for lane in REMOTE:
            part_copy(part, lane).wait_recv()
        for lane in range(LANES):
            tile = part_recv[part, lane]
            part_pick[2 * lane] = tile
            part_pick[2 * lane + 1] = pltpu.roll(tile, rows, 1)
        for lane in range(LANES):
            s = 2 * lane
            mine = part_pick[s]
            mate = jnp.where(first_half, part_pick[partner[s]], part_pick[partner[s + 1]])
            top = jnp.maximum(mine, mate)
            total = top + jnp.log(jnp.exp(mine - top) + jnp.exp(mate - top))
            used = jnp.where(first_half, filled[s], filled[s + 1])
            total = jnp.where(used > 0, total, UNUSED)
            row = jnp.where(first_half, terms[chosen[s], part], terms[chosen[s + 1], part])
            target = total_recv if lane == REACH else total_send
            target[part, lane] = jnp.where(row_id < HEADS_PER_PART, total, row)
        for lane in REMOTE:
            total_copy(part, lane).start()

    def gradients(part):
        slot_now = lax.rem(part, 3)
        for lane in REMOTE:
            total_copy(part, lane).wait_recv()
        for sub in range(HEADS_PER_PART):
            cols = pl.ds(pl.multiple_of(part * width + sub * 128, 128), 128)
            inner = slice(sub * 128, (sub + 1) * 128)
            bias_part = jnp.zeros((128, 128), jnp.float32)
            for lane in range(LANES):
                factor = jnp.exp(
                    tops[slot_now, lane, sub : sub + 1, :] - total_recv[part, lane, sub : sub + 1, :]
                )
                row = total_recv[part, lane, HEADS_PER_PART + sub : HEADS_PER_PART + sub + 1, :]
                weights = exps[slot_now, sub, lane] * factor
                grad_scores = weights * (grads[slot_now, sub, lane] - row)
                bias_part = bias_part + grad_scores
                weights_low = weights.astype(jnp.bfloat16).reshape(8, 16, 128)
                grad_low = grad_scores.astype(jnp.bfloat16)
                grad_tall = grad_low.T
                grad_low = grad_low.reshape(8, 16, 128)
                across = slice(lane * 128, (lane + 1) * 128)
                for b in range(blocks):
                    down = slice(b * 128, (b + 1) * 128)
                    mask = mask_row[lane, b][None]
                    w_wide[down, across] = (weights_low * mask).reshape(128, 128)
                    d_wide[down, across] = (grad_low * mask).reshape(128, 128)
                    d_tall[across, down] = grad_tall * mask_col[lane, b]
            dq = (plain_dot(d_tall[...], k_ref[:, cols]) * scaling).astype(jnp.bfloat16)
            for lane in range(LANES):
                target = dq_recv if lane == REACH else dq_send
                target[part, lane, :, inner] = dq[lane * 128 : (lane + 1) * 128]
            bias_turned = bias_part.T
            bias_sum[
                pl.ds(pl.multiple_of((part * HEADS_PER_PART + sub) * rows, rows), rows), :
            ] = bias_turned[0:rows] + bias_turned[rows : 2 * rows]
            queries = span_recv[part, :, 0, :, inner].reshape(LANES * 128, 128)
            cotangents = span_recv[part, :, 1, :, inner].reshape(LANES * 128, 128)
            kg_hold[part, :, inner] = plain_dot(d_wide[...], queries) * scaling
            vg_hold[part, :, inner] = plain_dot(w_wide[...], cotangents)
        for lane in REMOTE:
            dq_copy(part, lane).start()
        hold_copy(part, 0).start()
        hold_copy(part, 1).start()

    def gather(part):
        columns = pl.ds(pl.multiple_of(part * width, width), width)
        for lane in REMOTE:
            dq_copy(part, lane).wait_recv()
        for lane in range(LANES):
            for half in range(CAP):
                dq_pick[lane * CAP + half] = dq_recv[
                    part, lane, half * rows : (half + 1) * rows, :
                ].astype(jnp.float32)
        for span in range(spans):
            both = dq_pick[place[2 * span]] + dq_pick[place[2 * span + 1]]
            qg_ref[span, :, columns] = both.astype(jnp.bfloat16)

    def step(t, carry):
        @pl.when(t + AHEAD < parts)
        def _():
            pack(t + AHEAD)
            send_spans(t + AHEAD)

        @pl.when(t < parts)
        def _():
            score(t)

        @pl.when((t >= 1) & (t < parts + 1))
        def _():
            combine(t - 1)

        @pl.when((t >= 2) & (t < parts + 2))
        def _():
            gradients(t - 2)

        @pl.when(t >= 3)
        def _():
            gather(t - 3)

        return carry

    lax.fori_loop(0, parts + 3, step, 0)

    half_rows = bias_sum.shape[0] // 2
    core_copy = pltpu.make_async_remote_copy(
        src_ref=bias_sum.at[pl.ds(pl.multiple_of((1 - dp) * half_rows, half_rows), half_rows)],
        dst_ref=core_recv,
        send_sem=core_ss,
        recv_sem=core_rs,
        device_id=(1 - dp, me),
        device_id_type=MESH,
    )
    core_copy.start()
    core_copy.wait_recv()
    mine = pl.ds(pl.multiple_of(dp * half_rows, half_rows), half_rows)
    z_send[...] = (bias_sum[mine, :] + core_recv[...]).reshape(z_send.shape)
    started = [core_copy]
    stages = ((0, at_z, z_send, z_recv), (1, at_x, x_send, x_recv), (2, at_y, y_send, y_recv))
    for axis, at, held, landed in stages:
        copies = []
        for ahead in (1, 2, 3):
            other = (at + ahead) % 4
            copies.append(
                pltpu.make_async_remote_copy(
                    src_ref=held.at[other],
                    dst_ref=landed.at[ahead - 1],
                    send_sem=ring_ss.at[axis, ahead - 1],
                    recv_sem=ring_rs.at[axis, ahead - 1],
                    device_id=ring_peers[3 * (ahead - 1) + axis],
                    device_id_type=MESH,
                )
            )
            copies[-1].start()
        for copy in copies:
            copy.wait_recv()
        total = held[at] + landed[0] + landed[1] + landed[2]
        if axis == 0:
            x_send[...] = total.reshape(x_send.shape)
        elif axis == 1:
            y_send[...] = total.reshape(y_send.shape)
        else:
            bg_ref[...] = total
        started += copies
    for copy in started:
        copy.wait_send()
    for lane in REMOTE:
        meta_copy(lane).wait_send()

    def finish(part, carry):
        for lane in REMOTE:
            span_copy(part, lane).wait_send()
            part_copy(part, lane).wait_send()
            total_copy(part, lane).wait_send()
            dq_copy(part, lane).wait_send()
        hold_copy(part, 0).wait()
        hold_copy(part, 1).wait()
        return carry

    lax.fori_loop(0, parts, finish, 0)


def per_device(queries, outputs, out_grad, keys, values, owner, slot, pos_bias):
    spans, rows, feat = queries.shape
    blocks, block_len, _ = keys.shape
    heads = pos_bias.shape[0] // rows
    head_size = feat // heads
    parts = heads // HEADS_PER_PART
    width = HEADS_PER_PART * head_size
    seq_count = lax.axis_size("seq")
    key_count = blocks * block_len
    cfg = (spans, rows, seq_count, parts, blocks, head_size ** (-0.5))
    vmem = pl.BlockSpec(memory_space=pltpu.VMEM)
    smem = pl.BlockSpec(memory_space=pltpu.SMEM)
    anywhere = pl.BlockSpec(memory_space=pl.ANY)
    f32, bf16 = jnp.float32, jnp.bfloat16
    two = CAP * rows
    bias_rows = heads * rows
    dma = pltpu.SemaphoreType.DMA
    scratch = [
        pltpu.VMEM((LANES, 8, two), f32),
        pltpu.VMEM((LANES, 8, two), f32),
        pltpu.VMEM((LANES, blocks, 16, two), bf16),
        pltpu.VMEM((LANES, blocks, two, block_len), bf16),
        pltpu.VMEM((spans, parts, 8, two), f32),
        pltpu.VMEM((parts, LANES, 2, two, width), bf16),
        pltpu.VMEM((parts, LANES, 2, two, width), bf16),
        pltpu.VMEM((parts, LANES, 8, two), f32),
        pltpu.VMEM((parts, LANES, 8, two), f32),
        pltpu.VMEM((SLOTS, 8, two), f32),
        pltpu.VMEM((parts, LANES, 8, two), f32),
        pltpu.VMEM((parts, LANES, 8, two), f32),
        pltpu.VMEM((3, LANES, 8, two), f32),
        pltpu.VMEM((3, HEADS_PER_PART, LANES, block_len, two), f32),
        pltpu.VMEM((3, HEADS_PER_PART, LANES, block_len, two), f32),
        pltpu.VMEM((key_count, LANES * two), bf16),
        pltpu.VMEM((key_count, LANES * two), bf16),
        pltpu.VMEM((LANES * two, key_count), bf16),
        pltpu.VMEM((parts, LANES, two, width), bf16),
        pltpu.VMEM((parts, LANES, two, width), bf16),
        pltpu.VMEM((SLOTS, rows, width), f32),
        pltpu.VMEM((parts, key_count, width), f32),
        pltpu.VMEM((parts, key_count, width), f32),
        pltpu.VMEM((bias_rows, block_len), f32),
        pltpu.VMEM((bias_rows // 2, block_len), f32),
        pltpu.VMEM((4, bias_rows // 8, block_len), f32),
        pltpu.VMEM((3, bias_rows // 8, block_len), f32),
        pltpu.VMEM((4, bias_rows // 32, block_len), f32),
        pltpu.VMEM((3, bias_rows // 32, block_len), f32),
        pltpu.VMEM((4, bias_rows // 128, block_len), f32),
        pltpu.VMEM((3, bias_rows // 128, block_len), f32),
        dma((LANES,)),
        dma((LANES,)),
    ]
    scratch += [dma((parts, LANES)) for _ in range(8)]
    scratch += [dma((2, parts)), dma, dma, dma((3, 3)), dma((3, 3))]
    pair_work = SLOTS * rows * key_count * feat
    call = pl.pallas_call(
        functools.partial(kernel, cfg),
        out_shape=(
            jax.ShapeDtypeStruct((spans, rows, feat), bf16),
            jax.ShapeDtypeStruct((key_count, feat), f32),
            jax.ShapeDtypeStruct((key_count, feat), f32),
            jax.ShapeDtypeStruct((bias_rows // 128, block_len), f32),
        ),
        in_specs=[smem, smem] + [vmem] * 6,
        out_specs=(vmem, anywhere, anywhere, vmem),
        scratch_shapes=scratch,
        compiler_params=pltpu.CompilerParams(
            collective_id=0, has_side_effects=True, vmem_limit_bytes=56 * 2**20
        ),
        cost_estimate=pl.CostEstimate(
            flops=10 * pair_work, bytes_accessed=20 * 2**20, transcendentals=0
        ),
    )
    query_grad, key_grad, value_grad, bias_grad = call(
        owner,
        slot,
        queries,
        outputs,
        out_grad,
        keys.reshape(key_count, feat),
        values.reshape(key_count, feat),
        pos_bias,
    )
    return (
        query_grad,
        key_grad.reshape(blocks, block_len, feat),
        value_grad.reshape(blocks, block_len, feat),
        bias_grad,
    )


def solution(mesh):
    rows = P(("dp", "seq"), None, None)
    pairs = P(("dp", "seq"), None)
    return jax.shard_map(
        per_device,
        mesh=mesh,
        in_specs=(rows, rows, rows, rows, rows, pairs, pairs, P()),
        out_specs=(rows, rows, rows, pairs),
        check_vma=False,
    )
```

time: 793 us -> 175 us (0.22); the launches traced: 783 us -> 175 us
  waiting for transfers between devices: 311 us -> 0 us
  local copies, waits for them, and re-layouts: 203 us -> 12.4 us
  Pallas kernels: 0 us -> 161 us
  starting transfers between devices: 127 us -> 0 us
  matrix products: 118 us -> 0 us
  between operations: 14.8 us -> 0.64 us
  other arithmetic: 8.6 us -> 0 us
    unnamed x2 -> x0, waiting for transfers between devices: 218 us -> none
    pallas_call x0 -> x1, Pallas kernels: none -> 161 us  [per_device(): call(owner, slot, queries, outputs, out_grad, keys.reshape(key_count, fea...]
    ppermute x20 -> x0, starting transfers between devices: 127 us -> none  [passed_along(): return lax.ppermute(block, axis, route)]
    dot_general x25 -> x0, matrix products: 118 us -> none  [the longest x10 52.9 us: accumulate(): jnp.dot(onehot, flat_pieces, precision=lax.Precision.HIGHEST, preferred_e...]
    ppermute x20 -> x0, waiting for transfers between devices: 93.3 us -> none  [passed_along(): return lax.ppermute(block, axis, route)]
    unnamed x83 -> x10, local copies, waits for them, and re-layouts: 61.9 us -> 12.4 us
    scatter x2 -> x0, local copies, waits for them, and re-layouts: 30.7 us -> none  [the longest x1 15.4 us: per_device(): slot_values = jnp.zeros((slot_total, block_len, feat_width), jnp.float32)...]
    reshape x4 -> x0, local copies, waits for them, and re-layouts: 26.9 us -> none  [the longest x1 9.3 us: per_device(): pair_value_grad = jnp.einsum('chij,cihd->cjhd', weights_low, grad_heads,...]
  transfers between devices with their start and end apart: 21 -> 0, of which waited for: 7 -> 0; matrix products, arithmetic and copies ran while one was open for 27% -> 0% of each run, Pallas kernels for 0% -> 0%
where the time goes in v1:
time: 175 us
  Pallas kernels  161 us (92%)
  local copies, waits for them, and re-layouts  12.4 us (7%)
    pallas_call x1, Pallas kernels, per_device(): call(owner, slot, queries, outputs, out_grad, keys.reshape(key_count, fea...  161 us
    unnamed x10, local copies, waits for them, and re-layouts  12.4 us

profile of v1, /device:TPU:1, one launch (start us, length us, event | category | flops | bytes accessed | tf_op | source)
XLA Modules:
  0.0 174.6 jit_solution(16687682597725561074)
XLA Ops:
  0.6 1.3 copy.12.owner_ref
  2.0 1.3 copy.13.slot_ref
  3.3 161.5 %shard_map.111 = (bf16[4,64,2048]{2,1,0:T(8,128)(2,1)}, f32[512,2048]{1,0:T(8,128)}, f32[512,2048]{1,0:T(8,128)}, f32[8,128]{1,0:T(8,128)}) custom-call(s32[4,2]{1,0:T(4,128)} %copy.12.owner_ref, s32[4,2]{1,0:T(4,128)} %copy.13.slot_ref, bf16[4,64,2048]{2,1,0:T(8,128)(2,1)} %q_ref.1, bf16[4,64,2048]{2,1,0:T(8,128)(2,1)} %o_ref.1, ...), custom_call_target="tpu_custom_call" | custom-call | flops 6710886400 | bytes 20971520 | tf_op jit(solution)/shard_map/pallas_call | solution.py:529
  164.8 2.3 %copy.18 = bf16[4,64,2048]{2,1,0:T(8,128)(2,1)} copy(bf16[4,64,2048]{2,1,0:T(8,128)(2,1)} %get-tuple-element.16) | data formatting | bytes 2097152
  167.1 0.0 copy-start
  167.1 4.8 %copy.19 = f32[4,128,2048]{2,1,0:T(8,128)} copy(f32[4,128,2048]{2,1,0:T(8,128)} %bitcast.5) | data formatting | bytes 8388608
  171.9 0.0 copy-done
  171.9 0.0 copy-start.1
  171.9 2.0 %copy.20 = f32[4,128,2048]{2,1,0:T(8,128)} copy(f32[4,128,2048]{2,1,0:T(8,128)S(1)} %bitcast.4) | data formatting | bytes 8388608
  174.0 0.0 copy-done.1
  174.0 0.6 copy.21
Async XLA Ops:
  167.1 4.9 %copy-start = (f32[512,2048]{1,0:T(8,128)S(1)}, f32[512,2048]{1,0:T(8,128)}, u32[]{:S(2)}) copy-start(f32[512,2048]{1,0:T(8,128)} %get-tuple-element.10) | copy-start | bytes 12582916
  171.9 2.0 %copy-start.1 = (f32[8,128]{1,0:T(8,128)S(1)}, f32[8,128]{1,0:T(8,128)}, u32[]{:S(2)}) copy-start(f32[8,128]{1,0:T(8,128)} %get-tuple-element.19) | copy-start | bytes 12292

commit v2 on v1

v2 whole, which is shorter than its diff:
```python
import functools

import jax
import jax.numpy as jnp
from jax import lax
from jax.experimental import pallas as pl
from jax.experimental.pallas import tpu as pltpu
from jax.sharding import PartitionSpec as P

REACH = 2
CAP = 2
LANES = 2 * REACH + 1
SLOTS = LANES * CAP
HEADS_PER_PART = 2
AHEAD = 2
UNUSED = 1e30
MESH = pl.DeviceIdType.MESH
REMOTE = tuple(lane for lane in range(LANES) if lane != REACH)


def rows_dot(a, b):
    return lax.dot_general(a, b, (((1,), (1,)), ((), ())), preferred_element_type=jnp.float32)


def plain_dot(a, b):
    return jnp.dot(a, b, preferred_element_type=jnp.float32)


def kernel(
    cfg,
    owner_ref,
    slot_ref,
    q_hbm,
    o_hbm,
    g_hbm,
    k_hbm,
    v_hbm,
    bias_hbm,
    qg_ref,
    kg_ref,
    vg_ref,
    bg_ref,
    q_ref,
    o_ref,
    g_ref,
    k_ref,
    v_ref,
    bias_ref,
    meta_send,
    meta_recv,
    mask_row,
    mask_col,
    terms,
    q_send,
    q_recv,
    g_send,
    g_recv,
    part_send,
    part_recv,
    part_pick,
    total_send,
    total_recv,
    tops,
    exps,
    w_wide,
    d_wide,
    d_tall,
    dq_send,
    dq_recv,
    dq_pick,
    kg_hold,
    vg_hold,
    bias_sum,
    core_recv,
    z_send,
    z_recv,
    xy_send,
    xy_recv,
    load_sem,
    meta_ss,
    meta_rs,
    q_ss,
    q_rs,
    g_ss,
    g_rs,
    part_ss,
    part_rs,
    total_ss,
    total_rs,
    dq_ss,
    dq_rs,
    hold_sem,
    core_ss,
    core_rs,
    z_ss,
    z_rs,
    xy_ss,
    xy_rs,
):
    spans, rows, seq_count, parts, blocks, scaling = cfg
    width = HEADS_PER_PART * 128
    pairs = 2 * spans
    dp = lax.axis_index("dp")
    me = lax.axis_index("seq")
    at_z, at_x, at_y = me // 16, (me // 4) % 4, me % 4

    def owner_at(lane):
        return (dp, lax.rem(me + (lane - REACH) + seq_count, seq_count))

    def asker_at(lane):
        return (dp, lax.rem(me - (lane - REACH) + seq_count, seq_count))

    def along_z(z):
        return (dp, z * 16 + at_x * 4 + at_y)

    def across(turn):
        return (dp, at_z * 16 + ((at_x + turn // 4) % 4) * 4 + (at_y + turn % 4) % 4)

    inputs = (
        (q_hbm, q_ref),
        (g_hbm, g_ref),
        (k_hbm, k_ref),
        (bias_hbm, bias_ref),
        (o_hbm, o_ref),
        (v_hbm, v_ref),
    )
    loads = [
        pltpu.make_async_copy(far, near, load_sem.at[n]) for n, (far, near) in enumerate(inputs)
    ]
    load_q, load_g, load_k, load_bias, load_o, load_v = loads
    greeted = [owner_at(lane) for lane in REMOTE] + [across(turn) for turn in range(1, 16)]
    greeted += [along_z((at_z + turn) % 4) for turn in (1, 2, 3)] + [(1 - dp, me)]
    barrier = pltpu.get_barrier_semaphore()
    for device in greeted:
        pl.semaphore_signal(barrier, inc=1, device_id=device, device_id_type=MESH)
    for load in loads:
        load.start()

    lane_of = [
        lax.rem(owner_ref[p % 2, p // 2] - me + REACH + seq_count, seq_count) for p in range(pairs)
    ]
    place = []
    for p in range(pairs):
        rank = jnp.int32(0)
        for other in range(p):
            rank = rank + jnp.where(lane_of[other] == lane_of[p], 1, 0)
        place.append(jnp.minimum(lane_of[p] * CAP + rank, SLOTS - 1))
    chosen, filled, block_id, partner = [], [], [], []
    for s in range(SLOTS):
        pick, used, block, mate = jnp.int32(0), jnp.int32(0), jnp.int32(0), jnp.int32(0)
        for p in range(pairs):
            hit = place[p] == s
            pick = jnp.where(hit, p // 2, pick)
            used = jnp.where(hit, 1, used)
            block = jnp.where(hit, slot_ref[p % 2, p // 2], block)
            mate = jnp.where(hit, place[p ^ 1], mate)
        chosen.append(pick)
        filled.append(used)
        block_id.append(block)
        partner.append((mate // 2) * 2 + (mate + s) % 2)

    lane_id = lax.broadcasted_iota(jnp.int32, (8, 128), 1)
    row_id = lax.broadcasted_iota(jnp.int32, (8, 128), 0)
    first_half = lane_id < rows

    def to_owner(held, landed, sent, got, at, lane):
        return pltpu.make_async_remote_copy(
            src_ref=held.at[at],
            dst_ref=landed.at[at],
            send_sem=sent.at[at],
            recv_sem=got.at[at],
            device_id=owner_at(lane),
            device_id_type=MESH,
        )

    def to_asker(held, landed, sent, got, at, lane):
        return pltpu.make_async_remote_copy(
            src_ref=held.at[at],
            dst_ref=landed.at[at],
            send_sem=sent.at[at],
            recv_sem=got.at[at],
            device_id=asker_at(lane),
            device_id_type=MESH,
        )

    def meta_copy(lane):
        return to_owner(meta_send, meta_recv, meta_ss, meta_rs, lane, lane)

    def q_copy(part, lane):
        return to_owner(q_send, q_recv, q_ss, q_rs, (part, lane), lane)

    def g_copy(part, lane):
        return to_owner(g_send, g_recv, g_ss, g_rs, (part, lane), lane)

    def part_copy(part, lane):
        return to_asker(part_send, part_recv, part_ss, part_rs, (part, lane), lane)

    def total_copy(part, lane):
        return to_owner(total_send, total_recv, total_ss, total_rs, (part, lane), lane)

    def dq_copy(part, lane):
        return to_asker(dq_send, dq_recv, dq_ss, dq_rs, (part, lane), lane)

    def hold_copy(part, which):
        held, out = ((kg_hold, kg_ref), (vg_hold, vg_ref))[which]
        columns = pl.ds(pl.multiple_of(part * width, width), width)
        return pltpu.make_async_copy(held.at[part], out.at[:, columns], hold_sem.at[which, part])

    def core_copy(part):
        quarter = part % 4
        return pltpu.make_async_remote_copy(
            src_ref=bias_sum.at[part],
            dst_ref=core_recv.at[quarter],
            send_sem=core_ss.at[quarter],
            recv_sem=core_rs.at[quarter],
            device_id=(1 - dp, me),
            device_id_type=MESH,
        )

    def z_copy(quarter, turn):
        return pltpu.make_async_remote_copy(
            src_ref=z_send.at[quarter],
            dst_ref=z_recv.at[turn],
            send_sem=z_ss.at[quarter],
            recv_sem=z_rs.at[turn],
            device_id=along_z(quarter),
            device_id_type=MESH,
        )

    def xy_copy(turn):
        target = ((at_x + turn // 4) % 4) * 4 + (at_y + turn % 4) % 4
        return pltpu.make_async_remote_copy(
            src_ref=xy_send.at[target],
            dst_ref=xy_recv.at[turn],
            send_sem=xy_ss.at[turn],
            recv_sem=xy_rs.at[turn],
            device_id=across(turn),
            device_id_type=MESH,
        )

    def send_rows(part, source, held, landed, copy):
        columns = pl.ds(pl.multiple_of(part * width, width), width)
        for lane in range(LANES):
            target = landed if lane == REACH else held
            for half in range(CAP):
                target[part, lane, half * rows : (half + 1) * rows, :] = source[
                    chosen[lane * CAP + half], :, columns
                ]
        for lane in REMOTE:
            copy(part, lane).start()

    def send_q(part):
        send_rows(part, q_ref, q_send, q_recv, q_copy)

    def send_g(part):
        send_rows(part, g_ref, g_send, g_recv, g_copy)

    for lane in range(LANES):
        tile = jnp.where(first_half, block_id[2 * lane], block_id[2 * lane + 1])
        target = meta_recv if lane == REACH else meta_send
        target[lane] = tile.astype(jnp.float32)
    load_q.wait()
    pl.semaphore_wait(barrier, len(greeted))
    for lane in REMOTE:
        meta_copy(lane).start()
    for part in range(AHEAD):
        send_q(part)
    load_g.wait()
    load_o.wait()

    def span_terms(span, carry):
        wide_lane = lax.broadcasted_iota(jnp.int32, (rows, 128), 1)
        gathered = jnp.zeros((rows, 128), jnp.float32)
        for head in range(parts * HEADS_PER_PART):
            cols = slice(head * 128, (head + 1) * 128)
            product = g_ref[span, :, cols].astype(jnp.float32) * o_ref[span, :, cols].astype(
                jnp.float32
            )
            gathered = jnp.where(
                wide_lane == head, jnp.sum(product, axis=1, keepdims=True), gathered
            )
        turned = jnp.concatenate([gathered, gathered], axis=0).T
        for part in range(parts):
            first = part * HEADS_PER_PART
            terms[span, part, HEADS_PER_PART : 2 * HEADS_PER_PART, :] = turned[
                first : first + HEADS_PER_PART, :
            ]
        return carry

    lax.fori_loop(0, spans, span_terms, 0)
    load_k.wait()
    load_bias.wait()
    load_v.wait()

    for lane in REMOTE:
        meta_copy(lane).wait_recv()
    for lane in range(LANES):
        wide = jnp.broadcast_to(meta_recv[lane, 0:1, :], (128, 128))
        tall = wide.T
        for b in range(blocks):
            mask_row[lane, b] = jnp.where(wide[0:16] == b, 1.0, 0.0).astype(jnp.bfloat16)
            mask_col[lane, b] = jnp.where(tall == b, 1.0, 0.0).astype(jnp.bfloat16)

    def picked(products, ids):
        result = products[0:128]
        for b in range(1, blocks):
            result = jnp.where(ids == b, products[b * 128 : (b + 1) * 128], result)
        return result

    def score(part):
        slot_now = lax.rem(part, 3)
        for lane in REMOTE:
            q_copy(part, lane).wait_recv()
        for sub in range(HEADS_PER_PART):
            cols = pl.ds(pl.multiple_of(part * width + sub * 128, 128), 128)
            inner = slice(sub * 128, (sub + 1) * 128)
            key_rows = k_ref[:, cols]
            bias_rows = bias_ref[
                pl.ds(pl.multiple_of((part * HEADS_PER_PART + sub) * rows, rows), rows), :
            ]
            bias_turned = jnp.concatenate([bias_rows, bias_rows], axis=0).T
            for lane in range(LANES):
                ids = meta_recv[lane, 0:1, :]
                scores = (
                    picked(rows_dot(key_rows, q_recv[part, lane, :, inner]), ids) * scaling
                    + bias_turned
                )
                top = jnp.max(scores, axis=0, keepdims=True)
                lifted = jnp.exp(scores - top)
                exps[slot_now, sub, lane] = lifted
                tops[slot_now, lane, sub : sub + 1, :] = top
                target = part_recv if lane == REACH else part_send
                target[part, lane, sub : sub + 1, :] = top + jnp.log(
                    jnp.sum(lifted, axis=0, keepdims=True)
                )
        for lane in REMOTE:
            part_copy(part, lane).start()

    def combine(part):
        for lane in REMOTE:
            part_copy(part, lane).wait_recv()
        for lane in range(LANES):
            tile = part_recv[part, lane]
            part_pick[2 * lane] = tile
            part_pick[2 * lane + 1] = pltpu.roll(tile, rows, 1)
        for lane in range(LANES):
            s = 2 * lane
            mine = part_pick[s]
            mate = jnp.where(first_half, part_pick[partner[s]], part_pick[partner[s + 1]])
            top = jnp.maximum(mine, mate)
            total = top + jnp.log(jnp.exp(mine - top) + jnp.exp(mate - top))
            used = jnp.where(first_half, filled[s], filled[s + 1])
            total = jnp.where(used > 0, total, UNUSED)
            row = jnp.where(first_half, terms[chosen[s], part], terms[chosen[s + 1], part])
            target = total_recv if lane == REACH else total_send
            target[part, lane] = jnp.where(row_id < HEADS_PER_PART, total, row)
        for lane in REMOTE:
            total_copy(part, lane).start()

    def gradients(part):
        slot_now = lax.rem(part, 3)
        for lane in REMOTE:
            total_copy(part, lane).wait_recv()
            g_copy(part, lane).wait_recv()
        for sub in range(HEADS_PER_PART):
            cols = pl.ds(pl.multiple_of(part * width + sub * 128, 128), 128)
            inner = slice(sub * 128, (sub + 1) * 128)
            value_rows = v_ref[:, cols]
            bias_part = jnp.zeros((128, 128), jnp.float32)
            for lane in range(LANES):
                ids = meta_recv[lane, 0:1, :]
                grad_weights = picked(rows_dot(value_rows, g_recv[part, lane, :, inner]), ids)
                factor = jnp.exp(
                    tops[slot_now, lane, sub : sub + 1, :] - total_recv[part, lane, sub : sub + 1, :]
                )
                row = total_recv[part, lane, HEADS_PER_PART + sub : HEADS_PER_PART + sub + 1, :]
                weights = exps[slot_now, sub, lane] * factor
                grad_scores = weights * (grad_weights - row)
                bias_part = bias_part + grad_scores
                weights_low = weights.astype(jnp.bfloat16).reshape(8, 16, 128)
                grad_low = grad_scores.astype(jnp.bfloat16)
                grad_tall = grad_low.T
                grad_low = grad_low.reshape(8, 16, 128)
                beside = slice(lane * 128, (lane + 1) * 128)
                for b in range(blocks):
                    down = slice(b * 128, (b + 1) * 128)
                    mask = mask_row[lane, b][None]
                    w_wide[sub, down, beside] = (weights_low * mask).reshape(128, 128)
                    d_wide[sub, down, beside] = (grad_low * mask).reshape(128, 128)
                    d_tall[beside, down] = grad_tall * mask_col[lane, b]
            dq = (plain_dot(d_tall[...], k_ref[:, cols]) * scaling).astype(jnp.bfloat16)
            for lane in range(LANES):
                target = dq_recv if lane == REACH else dq_send
                target[part, lane, :, inner] = dq[lane * 128 : (lane + 1) * 128]
            bias_turned = bias_part.T
            bias_sum[part, sub * rows : (sub + 1) * rows, :] = (
                bias_turned[0:rows] + bias_turned[rows : 2 * rows]
            )
        for lane in REMOTE:
            dq_copy(part, lane).start()

        @pl.when(part // 4 != dp)
        def _():
            core_copy(part).start()

        for sub in range(HEADS_PER_PART):
            inner = slice(sub * 128, (sub + 1) * 128)
            queries = q_recv[part, :, :, inner].reshape(LANES * 128, 128)
            cotangents = g_recv[part, :, :, inner].reshape(LANES * 128, 128)
            kg_hold[part, :, inner] = plain_dot(d_wide[sub], queries) * scaling
            vg_hold[part, :, inner] = plain_dot(w_wide[sub], cotangents)
        hold_copy(part, 0).start()
        hold_copy(part, 1).start()

    def reduce_cores(part):
        quarter = part % 4

        @pl.when(part // 4 == dp)
        def _():
            core_copy(part).wait_recv()
            z_send[quarter] = bias_sum[part] + core_recv[quarter]

            @pl.when(quarter != at_z)
            def _():
                z_copy(quarter, (at_z - quarter + 4) % 4 - 1).start()

    def gather(part):
        columns = pl.ds(pl.multiple_of(part * width, width), width)
        for lane in REMOTE:
            dq_copy(part, lane).wait_recv()
        for lane in range(LANES):
            for half in range(CAP):
                dq_pick[lane * CAP + half] = dq_recv[
                    part, lane, half * rows : (half + 1) * rows, :
                ].astype(jnp.float32)
        for span in range(spans):
            both = dq_pick[place[2 * span]] + dq_pick[place[2 * span + 1]]
            qg_ref[span, :, columns] = both.astype(jnp.bfloat16)

    def step(t, carry):
        @pl.when(t + AHEAD < parts)
        def _():
            send_q(t + AHEAD)

        @pl.when(t < parts)
        def _():
            send_g(t)
            score(t)

        @pl.when((t >= 1) & (t < parts + 1))
        def _():
            combine(t - 1)

        @pl.when(t >= 2)
        def _():
            gradients(t - 2)

        @pl.when(t >= 3)
        def _():
            reduce_cores(t - 3)
            gather(t - 3)

        return carry

    lax.fori_loop(0, parts + 2, step, 0)

    reduce_cores(parts - 1)
    for turn in range(3):
        z_copy(at_z, turn).wait_recv()
    mine = z_send[at_z] + z_recv[0] + z_recv[1] + z_recv[2]
    xy_send[...] = mine.reshape(16, 8, 128)
    for turn in range(1, 16):
        xy_copy(turn).start()
    gather(parts - 1)
    for turn in range(1, 16):
        xy_copy(turn).wait_recv()
    total = xy_send[at_x * 4 + at_y]
    for turn in range(1, 16):
        total = total + xy_recv[turn]
    bg_ref[...] = total
    for turn in range(1, 16):
        xy_copy(turn).wait_send()
    for lane in REMOTE:
        meta_copy(lane).wait_send()

    def finish(part, carry):
        for lane in REMOTE:
            q_copy(part, lane).wait_send()
            g_copy(part, lane).wait_send()
            part_copy(part, lane).wait_send()
            total_copy(part, lane).wait_send()
            dq_copy(part, lane).wait_send()

        @pl.when(part // 4 != dp)
        def _():
            core_copy(part).wait_send()

        @pl.when((part // 4 == dp) & (part % 4 != at_z))
        def _():
            z_copy(part % 4, (at_z - part % 4 + 4) % 4 - 1).wait_send()

        hold_copy(part, 0).wait()
        hold_copy(part, 1).wait()
        return carry

    lax.fori_loop(0, parts, finish, 0)


def per_device(queries, outputs, out_grad, keys, values, owner, slot, pos_bias):
    spans, rows, feat = queries.shape
    blocks, block_len, _ = keys.shape
    heads = pos_bias.shape[0] // rows
    head_size = feat // heads
    parts = heads // HEADS_PER_PART
    width = HEADS_PER_PART * head_size
    seq_count = lax.axis_size("seq")
    key_count = blocks * block_len
    cfg = (spans, rows, seq_count, parts, blocks, head_size ** (-0.5))
    vmem = pl.BlockSpec(memory_space=pltpu.VMEM)
    smem = pl.BlockSpec(memory_space=pltpu.SMEM)
    anywhere = pl.BlockSpec(memory_space=pl.ANY)
    f32, bf16 = jnp.float32, jnp.bfloat16
    two = CAP * rows
    bias_rows = heads * rows
    dma = pltpu.SemaphoreType.DMA
    near = [queries, outputs, out_grad]
    scratch = [pltpu.VMEM(array.shape, array.dtype) for array in near]
    scratch += [
        pltpu.VMEM((key_count, feat), bf16),
        pltpu.VMEM((key_count, feat), bf16),
        pltpu.VMEM(pos_bias.shape, f32),
        pltpu.VMEM((LANES, 8, two), f32),
        pltpu.VMEM((LANES, 8, two), f32),
        pltpu.VMEM((LANES, blocks, 16, two), bf16),
        pltpu.VMEM((LANES, blocks, two, block_len), bf16),
        pltpu.VMEM((spans, parts, 8, two), f32),
        pltpu.VMEM((parts, LANES, two, width), bf16),
        pltpu.VMEM((parts, LANES, two, width), bf16),
        pltpu.VMEM((parts, LANES, two, width), bf16),
        pltpu.VMEM((parts, LANES, two, width), bf16),
        pltpu.VMEM((parts, LANES, 8, two), f32),
        pltpu.VMEM((parts, LANES, 8, two), f32),
        pltpu.VMEM((SLOTS, 8, two), f32),
        pltpu.VMEM((parts, LANES, 8, two), f32),
        pltpu.VMEM((parts, LANES, 8, two), f32),
        pltpu.VMEM((3, LANES, 8, two), f32),
        pltpu.VMEM((3, HEADS_PER_PART, LANES, block_len, two), f32),
        pltpu.VMEM((HEADS_PER_PART, key_count, LANES * two), bf16),
        pltpu.VMEM((HEADS_PER_PART, key_count, LANES * two), bf16),
        pltpu.VMEM((LANES * two, key_count), bf16),
        pltpu.VMEM((parts, LANES, two, width), bf16),
        pltpu.VMEM((parts, LANES, two, width), bf16),
        pltpu.VMEM((SLOTS, rows, width), f32),
        pltpu.VMEM((parts, key_count, width), f32),
        pltpu.VMEM((parts, key_count, width), f32),
        pltpu.VMEM((parts, bias_rows // parts, block_len), f32),
        pltpu.VMEM((4, bias_rows // parts, block_len), f32),
        pltpu.VMEM((4, bias_rows // parts, block_len), f32),
        pltpu.VMEM((3, bias_rows // parts, block_len), f32),
        pltpu.VMEM((16, bias_rows // 128, block_len), f32),
        pltpu.VMEM((16, bias_rows // 128, block_len), f32),
        dma((6,)),
        dma((LANES,)),
        dma((LANES,)),
    ]
    scratch += [dma((parts, LANES)) for _ in range(10)]
    scratch += [dma((2, parts)), dma((4,)), dma((4,)), dma((4,)), dma((3,)), dma((16,)), dma((16,))]
    pair_work = SLOTS * rows * key_count * feat
    call = pl.pallas_call(
        functools.partial(kernel, cfg),
        out_shape=(
            jax.ShapeDtypeStruct((spans, rows, feat), bf16),
            jax.ShapeDtypeStruct((key_count, feat), f32),
            jax.ShapeDtypeStruct((key_count, feat), f32),
            jax.ShapeDtypeStruct((bias_rows // 128, block_len), f32),
        ),
        in_specs=[smem, smem] + [anywhere] * 6,
        out_specs=(vmem, anywhere, anywhere, vmem),
        scratch_shapes=scratch,
        compiler_params=pltpu.CompilerParams(
            collective_id=0, has_side_effects=True, vmem_limit_bytes=56 * 2**20
        ),
        cost_estimate=pl.CostEstimate(
            flops=10 * pair_work, bytes_accessed=20 * 2**20, transcendentals=0
        ),
    )
    query_grad, key_grad, value_grad, bias_grad = call(
        owner.T,
        slot.T,
        queries,
        outputs,
        out_grad,
        keys.reshape(key_count, feat),
        values.reshape(key_count, feat),
        pos_bias,
    )
    return (
        query_grad,
        key_grad.reshape(blocks, block_len, feat),
        value_grad.reshape(blocks, block_len, feat),
        bias_grad,
    )


def solution(mesh):
    rows = P(("dp", "seq"), None, None)
    pairs = P(("dp", "seq"), None)
    return jax.shard_map(
        per_device,
        mesh=mesh,
        in_specs=(rows, rows, rows, rows, rows, pairs, pairs, P()),
        out_specs=(rows, rows, rows, pairs),
        check_vma=False,
    )
```

time: 175 us -> 151 us (0.86); the launches traced: 175 us -> 148 us
  Pallas kernels: 161 us -> 138 us
  local copies, waits for them, and re-layouts: 12.4 us -> 9.77 us
    pallas_call x1, Pallas kernels: 161 us -> 138 us  [per_device(): call(owner.T, slot.T, queries, outputs, out_grad, keys.reshape(key_count,...]
    unnamed x10 -> x8, local copies, waits for them, and re-layouts: 12.4 us -> 9.77 us
where the time goes in v2:
time: 151 us; the launch traced here: 148 us
  Pallas kernels  138 us (91%)
  local copies, waits for them, and re-layouts  9.77 us (6%)
    pallas_call x1, Pallas kernels, per_device(): call(owner.T, slot.T, queries, outputs, out_grad, keys.reshape(key_count,...  138 us
    unnamed x8, local copies, waits for them, and re-layouts  9.77 us

profile of v2, /device:TPU:1, one launch (start us, length us, event | category | flops | bytes accessed | tf_op | source)
XLA Modules:
  0.0 148.3 jit_solution(1898557937191518151)
XLA Ops:
  0.6 137.9 %shard_map.111 = (bf16[4,64,2048]{2,1,0:T(8,128)(2,1)}, f32[512,2048]{1,0:T(8,128)}, f32[512,2048]{1,0:T(8,128)}, f32[8,128]{1,0:T(8,128)}) custom-call(s32[2,4]{1,0:T(2,128)} %bitcast.10, s32[2,4]{1,0:T(2,128)} %bitcast.11, bf16[4,64,2048]{2,1,0:T(8,128)(2,1)} %q_hbm.1, bf16[4,64,2048]{2,1,0:T(8,128)(2,1)} %o_hbm.1, bf16[4,64,2048]{2,1,0:T(8,128)(2,1)} %g_hbm.1, ...), custom_call_target="tpu_custom_call" | custom-call | flops 6710886400 | bytes 20971520 | tf_op jit(solution)/shard_map/pallas_call | solution.py:587
  138.5 2.3 %copy.16 = bf16[4,64,2048]{2,1,0:T(8,128)(2,1)} copy(bf16[4,64,2048]{2,1,0:T(8,128)(2,1)} %get-tuple-element.16) | data formatting | bytes 2097152
  140.8 0.0 copy-start
  140.8 4.8 %copy.17 = f32[4,128,2048]{2,1,0:T(8,128)} copy(f32[4,128,2048]{2,1,0:T(8,128)} %bitcast.7) | data formatting | bytes 8388608
  145.7 0.0 copy-done
  145.7 0.0 copy-start.1
  145.7 2.0 %copy.18 = f32[4,128,2048]{2,1,0:T(8,128)} copy(f32[4,128,2048]{2,1,0:T(8,128)S(1)} %bitcast.6) | data formatting | bytes 8388608
  147.7 0.0 copy-done.1
  147.7 0.6 copy.19
Async XLA Ops:
  140.8 4.9 %copy-start = (f32[512,2048]{1,0:T(8,128)S(1)}, f32[512,2048]{1,0:T(8,128)}, u32[]{:S(2)}) copy-start(f32[512,2048]{1,0:T(8,128)} %get-tuple-element.10) | copy-start | bytes 12582916
  145.7 2.0 %copy-start.1 = (f32[8,128]{1,0:T(8,128)S(1)}, f32[8,128]{1,0:T(8,128)}, u32[]{:S(2)}) copy-start(f32[8,128]{1,0:T(8,128)} %get-tuple-element.19) | copy-start | bytes 12292

commit v3 on v2

--- a/solution.py
+++ b/solution.py
@@ -13,9 +13,12 @@
 SLOTS = LANES * CAP
 HEADS_PER_PART = 2
 AHEAD = 2
+FAR_AHEAD = 4
 UNUSED = 1e30
 MESH = pl.DeviceIdType.MESH
 REMOTE = tuple(lane for lane in range(LANES) if lane != REACH)
+NEAR = (REACH - 1, REACH + 1)
+FAR = (0, LANES - 1)
 
 
 def rows_dot(a, b):
@@ -68,8 +71,6 @@
     dq_send,
     dq_recv,
     dq_pick,
-    kg_hold,
-    vg_hold,
     bias_sum,
     core_recv,
     z_send,
@@ -89,7 +90,6 @@
     total_rs,
     dq_ss,
     dq_rs,
-    hold_sem,
     core_ss,
     core_rs,
     z_ss,
@@ -201,11 +201,6 @@
     def dq_copy(part, lane):
         return to_asker(dq_send, dq_recv, dq_ss, dq_rs, (part, lane), lane)
 
-    def hold_copy(part, which):
-        held, out = ((kg_hold, kg_ref), (vg_hold, vg_ref))[which]
-        columns = pl.ds(pl.multiple_of(part * width, width), width)
-        return pltpu.make_async_copy(held.at[part], out.at[:, columns], hold_sem.at[which, part])
-
     def core_copy(part):
         quarter = part % 4
         return pltpu.make_async_remote_copy(
@@ -238,22 +233,23 @@
             device_id_type=MESH,
         )
 
-    def send_rows(part, source, held, landed, copy):
+    def send_rows(part, source, held, landed, copy, lanes):
         columns = pl.ds(pl.multiple_of(part * width, width), width)
-        for lane in range(LANES):
+        for lane in lanes:
             target = landed if lane == REACH else held
             for half in range(CAP):
                 target[part, lane, half * rows : (half + 1) * rows, :] = source[
                     chosen[lane * CAP + half], :, columns
                 ]
-        for lane in REMOTE:
-            copy(part, lane).start()
-
-    def send_q(part):
-        send_rows(part, q_ref, q_send, q_recv, q_copy)
-
-    def send_g(part):
-        send_rows(part, g_ref, g_send, g_recv, g_copy)
+        for lane in lanes:
+            if lane != REACH:
+                copy(part, lane).start()
+
+    def send_q(part, lanes):
+        send_rows(part, q_ref, q_send, q_recv, q_copy, lanes)
+
+    def send_g(part, lanes):
+        send_rows(part, g_ref, g_send, g_recv, g_copy, lanes)
 
     for lane in range(LANES):
         tile = jnp.where(first_half, block_id[2 * lane], block_id[2 * lane + 1])
@@ -264,8 +260,19 @@
     for lane in REMOTE:
         meta_copy(lane).start()
     for part in range(AHEAD):
-        send_q(part)
+        send_q(part, FAR)
+        send_q(part, NEAR + (REACH,))
     load_g.wait()
+
+    def send_far(part, carry):
+        @pl.when(part < parts)
+        def _():
+            send_q(part, FAR)
+
+        send_g(part - AHEAD, FAR)
+        return carry
+
+    lax.fori_loop(AHEAD, AHEAD + FAR_AHEAD, send_far, 0)
     load_o.wait()
 
     def span_terms(span, carry):
@@ -407,10 +414,9 @@
             inner = slice(sub * 128, (sub + 1) * 128)
             queries = q_recv[part, :, :, inner].reshape(LANES * 128, 128)
             cotangents = g_recv[part, :, :, inner].reshape(LANES * 128, 128)
-            kg_hold[part, :, inner] = plain_dot(d_wide[sub], queries) * scaling
-            vg_hold[part, :, inner] = plain_dot(w_wide[sub], cotangents)
-        hold_copy(part, 0).start()
-        hold_copy(part, 1).start()
+            cols = pl.ds(pl.multiple_of(part * width + sub * 128, 128), 128)
+            kg_ref[:, cols] = plain_dot(d_wide[sub], queries) * scaling
+            vg_ref[:, cols] = plain_dot(w_wide[sub], cotangents)
 
     def reduce_cores(part):
         quarter = part % 4
@@ -438,13 +444,17 @@
             qg_ref[span, :, columns] = both.astype(jnp.bfloat16)
 
     def step(t, carry):
+        @pl.when(t + FAR_AHEAD < parts)
+        def _():
+            send_far(t + FAR_AHEAD + AHEAD, 0)
+
         @pl.when(t + AHEAD < parts)
         def _():
-            send_q(t + AHEAD)
+            send_q(t + AHEAD, NEAR + (REACH,))
 
         @pl.when(t < parts)
         def _():
-            send_g(t)
+            send_g(t, NEAR + (REACH,))
             score(t)
 
         @pl.when((t >= 1) & (t < parts + 1))
@@ -499,11 +509,18 @@
         def _():
             z_copy(part % 4, (at_z - part % 4 + 4) % 4 - 1).wait_send()
 
-        hold_copy(part, 0).wait()
-        hold_copy(part, 1).wait()
         return carry
 
     lax.fori_loop(0, parts, finish, 0)
+
+
+def store(*refs):
+    sem = refs[8]
+    copies = [pltpu.make_async_copy(refs[n], refs[4 + n], sem.at[n]) for n in range(4)]
+    for copy in copies:
+        copy.start()
+    for copy in copies:
+        copy.wait()
 
 
 def per_device(queries, outputs, out_grad, keys, values, owner, slot, pos_bias):
@@ -551,8 +568,6 @@
         pltpu.VMEM((parts, LANES, two, width), bf16),
         pltpu.VMEM((parts, LANES, two, width), bf16),
         pltpu.VMEM((SLOTS, rows, width), f32),
-        pltpu.VMEM((parts, key_count, width), f32),
-        pltpu.VMEM((parts, key_count, width), f32),
         pltpu.VMEM((parts, bias_rows // parts, block_len), f32),
         pltpu.VMEM((4, bias_rows // parts, block_len), f32),
         pltpu.VMEM((4, bias_rows // parts, block_len), f32),
@@ -564,27 +579,27 @@
         dma((LANES,)),
     ]
     scratch += [dma((parts, LANES)) for _ in range(10)]
-    scratch += [dma((2, parts)), dma((4,)), dma((4,)), dma((4,)), dma((3,)), dma((16,)), dma((16,))]
+    scratch += [dma((4,)), dma((4,)), dma((4,)), dma((3,)), dma((16,)), dma((16,))]
     pair_work = SLOTS * rows * key_count * feat
     call = pl.pallas_call(
         functools.partial(kernel, cfg),
         out_shape=(
-            jax.ShapeDtypeStruct((spans, rows, feat), bf16),
-            jax.ShapeDtypeStruct((key_count, feat), f32),
-            jax.ShapeDtypeStruct((key_count, feat), f32),
-            jax.ShapeDtypeStruct((bias_rows // 128, block_len), f32),
+            pltpu.VMEM((spans, rows, feat), bf16),
+            pltpu.VMEM((key_count, feat), f32),
+            pltpu.VMEM((key_count, feat), f32),
+            pltpu.VMEM((bias_rows // 128, block_len), f32),
         ),
         in_specs=[smem, smem] + [anywhere] * 6,
-        out_specs=(vmem, anywhere, anywhere, vmem),
+        out_specs=(vmem, vmem, vmem, vmem),
         scratch_shapes=scratch,
         compiler_params=pltpu.CompilerParams(
-            collective_id=0, has_side_effects=True, vmem_limit_bytes=56 * 2**20
+            collective_id=0, has_side_effects=True, vmem_limit_bytes=46 * 2**20
         ),
         cost_estimate=pl.CostEstimate(
             flops=10 * pair_work, bytes_accessed=20 * 2**20, transcendentals=0
         ),
     )
-    query_grad, key_grad, value_grad, bias_grad = call(
+    results = call(
         owner.T,
         slot.T,
         queries,
@@ -594,6 +609,14 @@
         values.reshape(key_count, feat),
         pos_bias,
     )
+    query_grad, key_grad, value_grad, bias_grad = pl.pallas_call(
+        store,
+        out_shape=tuple(jax.ShapeDtypeStruct(r.shape, r.dtype) for r in results),
+        in_specs=[vmem] * 4,
+        out_specs=(anywhere,) * 4,
+        scratch_shapes=[dma((4,))],
+        compiler_params=pltpu.CompilerParams(vmem_limit_bytes=2**20),
+    )(*results)
     return (
         query_grad,
         key_grad.reshape(blocks, block_len, feat),

time: 151 us -> 140 us (0.927)
  local copies, waits for them, and re-layouts: 9.77 us -> 0 us
    unnamed x8 -> x0, local copies, waits for them, and re-layouts: 9.77 us -> none
    pallas_call x1, Pallas kernels: 138 us -> 133 us  [per_device(): call(owner.T, slot.T, queries, outputs, out_grad, keys.reshape(key_count,...]
    pallas_call x0 -> x1, Pallas kernels: none -> 3.78 us  [per_device(): pl.pallas_call(store, out_shape=tuple((jax.ShapeDtypeStruct(r.shape, r.dt...]
where the time goes in v3:
time: 140 us; the launch traced here: 138 us
  Pallas kernels  137 us (98%)
    pallas_call x1, Pallas kernels, per_device(): call(owner.T, slot.T, queries, outputs, out_grad, keys.reshape(key_count,...  133 us
    pallas_call x1, Pallas kernels, per_device(): pl.pallas_call(store, out_shape=tuple((jax.ShapeDtypeStruct(r.shape, r.dt...  3.78 us

profile of v3, /device:TPU:1, one launch (start us, length us, event | category | flops | bytes accessed | tf_op | source)
XLA Modules:
  0.0 137.7 jit_solution(9440372822081195420)
XLA Ops:
  0.6 133.3 %shard_map.111 = (bf16[4,64,2048]{2,1,0:T(8,128)(2,1)S(1)}, f32[512,2048]{1,0:T(8,128)S(1)}, f32[512,2048]{1,0:T(8,128)S(1)}, f32[8,128]{1,0:T(8,128)S(1)}) custom-call(s32[2,4]{1,0:T(2,128)} %bitcast.10, s32[2,4]{1,0:T(2,128)} %bitcast.11, bf16[4,64,2048]{2,1,0:T(8,128)(2,1)} %q_hbm.1, bf16[4,64,2048]{2,1,0:T(8,128)(2,1)} %o_hbm.1, ...), custom_call_target="tpu_custom_call" | custom-call | flops 6710886400 | bytes 20971520 | tf_op jit(solution)/shard_map/pallas_call | solution.py:602
  133.9 3.8 %shard_map.112 = (bf16[4,64,2048]{2,1,0:T(8,128)(2,1)}, f32[512,2048]{1,0:T(8,128)}, f32[512,2048]{1,0:T(8,128)}, f32[8,128]{1,0:T(8,128)}) custom-call(bf16[4,64,2048]{2,1,0:T(8,128)(2,1)S(1)} %get-tuple-element.12.refs_0_, f32[512,2048]{1,0:T(8,128)S(1)} %get-tuple-element.13.refs_1_, f32[512,2048]{1,0:T(8,128)S(1)} %get-tuple-element.14.refs_2_, ...), custom_call_target="tpu_custom_call" | custom-call | tf_op jit(solution)/shard_map/pallas_call | solution.py:612

commit v4 on v3

--- a/solution.py
+++ b/solution.py
@@ -14,6 +14,7 @@
 HEADS_PER_PART = 2
 AHEAD = 2
 FAR_AHEAD = 4
+HELD = 1
 UNUSED = 1e30
 MESH = pl.DeviceIdType.MESH
 REMOTE = tuple(lane for lane in range(LANES) if lane != REACH)
@@ -233,7 +234,7 @@
             device_id_type=MESH,
         )
 
-    def send_rows(part, source, held, landed, copy, lanes):
+    def pack(part, source, held, landed, lanes):
         columns = pl.ds(pl.multiple_of(part * width, width), width)
         for lane in lanes:
             target = landed if lane == REACH else held
@@ -241,27 +242,33 @@
                 target[part, lane, half * rows : (half + 1) * rows, :] = source[
                     chosen[lane * CAP + half], :, columns
                 ]
+
+    def start(part, copy, lanes):
         for lane in lanes:
             if lane != REACH:
                 copy(part, lane).start()
 
     def send_q(part, lanes):
-        send_rows(part, q_ref, q_send, q_recv, q_copy, lanes)
+        pack(part, q_ref, q_send, q_recv, lanes)
+        start(part, q_copy, lanes)
 
     def send_g(part, lanes):
-        send_rows(part, g_ref, g_send, g_recv, g_copy, lanes)
+        pack(part, g_ref, g_send, g_recv, lanes)
+        start(part, g_copy, lanes)
 
     for lane in range(LANES):
         tile = jnp.where(first_half, block_id[2 * lane], block_id[2 * lane + 1])
         target = meta_recv if lane == REACH else meta_send
         target[lane] = tile.astype(jnp.float32)
+    part_pick[...] = jnp.zeros(part_pick.shape, jnp.float32)
     load_q.wait()
+    for part in range(AHEAD):
+        pack(part, q_ref, q_send, q_recv, range(LANES))
     pl.semaphore_wait(barrier, len(greeted))
     for lane in REMOTE:
         meta_copy(lane).start()
     for part in range(AHEAD):
-        send_q(part, FAR)
-        send_q(part, NEAR + (REACH,))
+        start(part, q_copy, FAR + NEAR)
     load_g.wait()
 
     def send_far(part, carry):
@@ -347,9 +354,8 @@
         for lane in REMOTE:
             part_copy(part, lane).wait_recv()
         for lane in range(LANES):
-            tile = part_recv[part, lane]
-            part_pick[2 * lane] = tile
-            part_pick[2 * lane + 1] = pltpu.roll(tile, rows, 1)
+            part_pick[2 * lane, 0:HEADS_PER_PART, :] = part_recv[part, lane]
+            part_pick[2 * lane + 1] = pltpu.roll(part_pick[2 * lane], rows, 1)
         for lane in range(LANES):
             s = 2 * lane
             mine = part_pick[s]
@@ -360,15 +366,31 @@
             total = jnp.where(used > 0, total, UNUSED)
             row = jnp.where(first_half, terms[chosen[s], part], terms[chosen[s + 1], part])
             target = total_recv if lane == REACH else total_send
-            target[part, lane] = jnp.where(row_id < HEADS_PER_PART, total, row)
+            target[part, lane] = jnp.where(row_id < HEADS_PER_PART, total, row)[
+                0 : 2 * HEADS_PER_PART
+            ]
         for lane in REMOTE:
             total_copy(part, lane).start()
+
+    def send_dq(part, carry):
+        for lane in REMOTE:
+            dq_copy(part, lane).start()
+        return carry
 
     def gradients(part):
         slot_now = lax.rem(part, 3)
         for lane in REMOTE:
             total_copy(part, lane).wait_recv()
             g_copy(part, lane).wait_recv()
+
+        @pl.when(part >= HELD + 1)
+        def _():
+            send_dq(part - HELD - 1, 0)
+
+        @pl.when(part == parts - 1)
+        def _():
+            lax.fori_loop(parts - 1 - HELD, parts - 1, send_dq, 0)
+
         for sub in range(HEADS_PER_PART):
             cols = pl.ds(pl.multiple_of(part * width + sub * 128, 128), 128)
             inner = slice(sub * 128, (sub + 1) * 128)
@@ -403,8 +425,9 @@
             bias_sum[part, sub * rows : (sub + 1) * rows, :] = (
                 bias_turned[0:rows] + bias_turned[rows : 2 * rows]
             )
-        for lane in REMOTE:
-            dq_copy(part, lane).start()
+        @pl.when(part == parts - 1)
+        def _():
+            send_dq(part, 0)
 
         @pl.when(part // 4 != dp)
         def _():
@@ -430,7 +453,7 @@
             def _():
                 z_copy(quarter, (at_z - quarter + 4) % 4 - 1).start()
 
-    def gather(part):
+    def gather(part, carry):
         columns = pl.ds(pl.multiple_of(part * width, width), width)
         for lane in REMOTE:
             dq_copy(part, lane).wait_recv()
@@ -442,6 +465,7 @@
         for span in range(spans):
             both = dq_pick[place[2 * span]] + dq_pick[place[2 * span + 1]]
             qg_ref[span, :, columns] = both.astype(jnp.bfloat16)
+        return carry
 
     def step(t, carry):
         @pl.when(t + FAR_AHEAD < parts)
@@ -468,7 +492,10 @@
         @pl.when(t >= 3)
         def _():
             reduce_cores(t - 3)
-            gather(t - 3)
+
+        @pl.when(t >= HELD + 4)
+        def _():
+            gather(t - HELD - 4, 0)
 
         return carry
 
@@ -481,7 +508,7 @@
     xy_send[...] = mine.reshape(16, 8, 128)
     for turn in range(1, 16):
         xy_copy(turn).start()
-    gather(parts - 1)
+    lax.fori_loop(parts - HELD - 2, parts, gather, 0)
     for turn in range(1, 16):
         xy_copy(turn).wait_recv()
     total = xy_send[at_x * 4 + at_y]
@@ -555,11 +582,11 @@
         pltpu.VMEM((parts, LANES, two, width), bf16),
         pltpu.VMEM((parts, LANES, two, width), bf16),
         pltpu.VMEM((parts, LANES, two, width), bf16),
-        pltpu.VMEM((parts, LANES, 8, two), f32),
-        pltpu.VMEM((parts, LANES, 8, two), f32),
+        pltpu.VMEM((parts, LANES, HEADS_PER_PART, two), f32),
+        pltpu.VMEM((parts, LANES, HEADS_PER_PART, two), f32),
         pltpu.VMEM((SLOTS, 8, two), f32),
-        pltpu.VMEM((parts, LANES, 8, two), f32),
-        pltpu.VMEM((parts, LANES, 8, two), f32),
+        pltpu.VMEM((parts, LANES, 2 * HEADS_PER_PART, two), f32),
+        pltpu.VMEM((parts, LANES, 2 * HEADS_PER_PART, two), f32),
         pltpu.VMEM((3, LANES, 8, two), f32),
         pltpu.VMEM((3, HEADS_PER_PART, LANES, block_len, two), f32),
         pltpu.VMEM((HEADS_PER_PART, key_count, LANES * two), bf16),

time: 140 us -> 136 us (0.971)
  Pallas kernels: 137 us -> 134 us
    pallas_call x1, Pallas kernels: 133 us -> 130 us  [per_device(): call(owner.T, slot.T, queries, outputs, out_grad, keys.reshape(key_count,...]
where the time goes in v4:
time: 136 us; the launch traced here: 134 us
  Pallas kernels  134 us (99%)
    pallas_call x1, Pallas kernels, per_device(): call(owner.T, slot.T, queries, outputs, out_grad, keys.reshape(key_count,...  130 us
    pallas_call x1, Pallas kernels, per_device(): pl.pallas_call(store, out_shape=tuple((jax.ShapeDtypeStruct(r.shape, r.dt...  3.78 us

profile of v4, /device:TPU:1, one launch (start us, length us, event | category | flops | bytes accessed | tf_op | source)
XLA Modules:
  0.0 134.2 jit_solution(7269901034581818473)
XLA Ops:
  0.6 129.8 %shard_map.111 = (bf16[4,64,2048]{2,1,0:T(8,128)(2,1)S(1)}, f32[512,2048]{1,0:T(8,128)S(1)}, f32[512,2048]{1,0:T(8,128)S(1)}, f32[8,128]{1,0:T(8,128)S(1)}) custom-call(s32[2,4]{1,0:T(2,128)} %bitcast.10, s32[2,4]{1,0:T(2,128)} %bitcast.11, bf16[4,64,2048]{2,1,0:T(8,128)(2,1)} %q_hbm.1, bf16[4,64,2048]{2,1,0:T(8,128)(2,1)} %o_hbm.1, ...), custom_call_target="tpu_custom_call" | custom-call | flops 6710886400 | bytes 20971520 | tf_op jit(solution)/shard_map/pallas_call | solution.py:629
  130.4 3.8 %shard_map.112 = (bf16[4,64,2048]{2,1,0:T(8,128)(2,1)}, f32[512,2048]{1,0:T(8,128)}, f32[512,2048]{1,0:T(8,128)}, f32[8,128]{1,0:T(8,128)}) custom-call(bf16[4,64,2048]{2,1,0:T(8,128)(2,1)S(1)} %get-tuple-element.12.refs_0_, f32[512,2048]{1,0:T(8,128)S(1)} %get-tuple-element.13.refs_1_, f32[512,2048]{1,0:T(8,128)S(1)} %get-tuple-element.14.refs_2_, ...), custom_call_target="tpu_custom_call" | custom-call | tf_op jit(solution)/shard_map/pallas_call | solution.py:639

commit v5 on v4

--- a/solution.py
+++ b/solution.py
@@ -12,7 +12,7 @@
 LANES = 2 * REACH + 1
 SLOTS = LANES * CAP
 HEADS_PER_PART = 2
-AHEAD = 2
+AHEAD = 1
 FAR_AHEAD = 4
 HELD = 1
 UNUSED = 1e30

time: 136 us -> 135 us (level)
  no operation moved by 1% of the time
where the time goes in v5:
time: 135 us; the launch traced here: 134 us
  Pallas kernels  133 us (99%)
    pallas_call x1, Pallas kernels, per_device(): call(owner.T, slot.T, queries, outputs, out_grad, keys.reshape(key_count,...  129 us
    pallas_call x1, Pallas kernels, per_device(): pl.pallas_call(store, out_shape=tuple((jax.ShapeDtypeStruct(r.shape, r.dt...  3.78 us

profile of v5, /device:TPU:1, one launch (start us, length us, event | category | flops | bytes accessed | tf_op | source)
XLA Modules:
  0.0 133.5 jit_solution(13167338819865994471)
XLA Ops:
  0.6 129.1 %shard_map.111 = (bf16[4,64,2048]{2,1,0:T(8,128)(2,1)S(1)}, f32[512,2048]{1,0:T(8,128)S(1)}, f32[512,2048]{1,0:T(8,128)S(1)}, f32[8,128]{1,0:T(8,128)S(1)}) custom-call(s32[2,4]{1,0:T(2,128)} %bitcast.10, s32[2,4]{1,0:T(2,128)} %bitcast.11, bf16[4,64,2048]{2,1,0:T(8,128)(2,1)} %q_hbm.1, bf16[4,64,2048]{2,1,0:T(8,128)(2,1)} %o_hbm.1, ...), custom_call_target="tpu_custom_call" | custom-call | flops 6710886400 | bytes 20971520 | tf_op jit(solution)/shard_map/pallas_call | solution.py:629
  129.7 3.8 %shard_map.112 = (bf16[4,64,2048]{2,1,0:T(8,128)(2,1)}, f32[512,2048]{1,0:T(8,128)}, f32[512,2048]{1,0:T(8,128)}, f32[8,128]{1,0:T(8,128)}) custom-call(bf16[4,64,2048]{2,1,0:T(8,128)(2,1)S(1)} %get-tuple-element.12.refs_0_, f32[512,2048]{1,0:T(8,128)S(1)} %get-tuple-element.13.refs_1_, f32[512,2048]{1,0:T(8,128)S(1)} %get-tuple-element.14.refs_2_, ...), custom_call_target="tpu_custom_call" | custom-call | tf_op jit(solution)/shard_map/pallas_call | solution.py:639
